TPU v7x, 32 devices: a whole 2x2x4 slice. The times are simulated.
32 devices in a mesh: dp: 4 (over z), row: 4 (over y, x), col: 2 (over core).
Axes of the slice: x: 2, y: 2, z: 4, core: 2. Of those that a mesh axis runs over, the one named last changes fastest.
Arguments:
- tokens: bfloat16 [16384, 512], P(('dp', 'row'), 'col'), may hold values from -7.2 to 7.2
- cotangent: bfloat16 [16384, 512], P(('dp', 'row'), 'col'), may hold values from -6 to 6
- qkv_weight: float32 [3, 512, 512], P(None, 'row', 'col'), may hold values from -0.25 to 0.25
- proj_weight: float32 [512, 512], P('col', 'row'), may hold values from -3 to 3
- up_weight: float32 [512, 2048], P('row', 'col'), may hold values from -0.25 to 0.25
- down_weight: float32 [2048, 512], P('col', 'row'), may hold values from -0.125 to 0.125
- vectors: float32 [12, 512], P(None, 'col'), may hold values from -0.9 to 3.25, as said below
- qkv_mean: float32 [3, 512, 512], P(None, 'row', 'col'), may hold values from -80 to 80
- qkv_square: float32 [3, 512, 512], P(None, 'row', 'col'), may hold values from 8.192 to 131.072
- proj_mean: float32 [512, 512], P('col', 'row'), may hold values from -6 to 6
- proj_square: float32 [512, 512], P('col', 'row'), may hold values from 0.08192 to 1.31072
- up_mean: float32 [512, 2048], P('row', 'col'), may hold values from -32 to 32
- up_square: float32 [512, 2048], P('row', 'col'), may hold values from 0.98304 to 16.384
- down_mean: float32 [2048, 512], P('col', 'row'), may hold values from -48 to 48
- down_square: float32 [2048, 512], P('col', 'row'), may hold values from 2.94912 to 47.5136
- vector_mean: float32 [12, 512], P(None, 'col'), may hold values from -80 to 80
- vector_square: float32 [12, 512], P(None, 'col'), may hold values from 8.192 to 131.072
Outputs:
- block_out: bfloat16 [16384, 512], P(('dp', 'row'), 'col')
- input_grad: float32 [16384, 512], P(('dp', 'row'), 'col')
- qkv_new: float32 [3, 512, 512], P(None, 'row', 'col')
- qkv_mean_new: float32 [3, 512, 512], P(None, 'row', 'col')
- qkv_square_new: float32 [3, 512, 512], P(None, 'row', 'col')
- proj_new: float32 [512, 512], P('col', 'row')
- proj_mean_new: float32 [512, 512], P('col', 'row')
- proj_square_new: float32 [512, 512], P('col', 'row')
- up_new: float32 [512, 2048], P('row', 'col')
- up_mean_new: float32 [512, 2048], P('row', 'col')
- up_square_new: float32 [512, 2048], P('row', 'col')
- down_new: float32 [2048, 512], P('col', 'row')
- down_mean_new: float32 [2048, 512], P('col', 'row')
- down_square_new: float32 [2048, 512], P('col', 'row')
- vector_new: float32 [12, 512], P(None, 'col')
- vector_mean_new: float32 [12, 512], P(None, 'col')
- vector_square_new: float32 [12, 512], P(None, 'col')
- vector_grad: float32 [12, 512], P(None, 'col')
Inputs may be any that keep to these rules, and one draw needn't show every extreme that they name: `vectors`: rows 4 and 6 are positive.
All inputs are finite; a program needn't handle non-finite values.
Results may differ from a plain program's by a relative error of at most 0.013.
The roundings to bfloat16 on the way count: a program that leaves them out, or rounds other values in their place, can miss the bound.
Values may be sent and summed in bfloat16 or wider, within the bound.
A program may use at most 128 MiB of HBM per device.

v0:
```python
from functools import partial

import jax
import jax.numpy as jnp
from jax import lax
from jax.sharding import PartitionSpec as P

D = 512
HEAD_DIM = 64
SEQ = 512
STEP = 10


NORM_EPS = 1e-05
BETA_ONE = 0.9
BETA_TWO = 0.999
ADAM_EPS = 1e-08
DECAY_RATE = 0.01
RATE_QKV = 0.03
RATE_PROJ = 0.3
RATE_UP = 0.03
RATE_DOWN = 0.02
RATE_VECTOR = 0.3


def matmul(left, right):
    return jnp.dot(left, right, preferred_element_type=jnp.float32)


def left_contract(left, right):
    return lax.dot_general(
        left, right, (((0,), (0,)), ((), ())), preferred_element_type=jnp.float32
    )


def right_contract(left, right):
    return lax.dot_general(
        left, right, (((1,), (1,)), ((), ())), preferred_element_type=jnp.float32
    )


def gather_features(summed):
    return lax.all_gather(summed, "col", axis=1, tiled=True)


def gather_grads(summed):
    return lax.all_gather(summed, "col", axis=1, tiled=True)


def sum_partial(summed):
    return lax.psum_scatter(summed, "col", scatter_dimension=1, tiled=True)


def sum_grad_partial(summed):
    return lax.psum_scatter(summed, "col", scatter_dimension=1, tiled=True)


def normalize(summed, gain_row, shift_row):
    mean_row = (lax.psum(jnp.sum(summed, -1), "col") / D)[:, None]
    centered = summed - mean_row
    variance = (lax.psum(jnp.sum(centered * centered, -1), "col") / D)[:, None]
    scaling = lax.rsqrt(variance + NORM_EPS)
    normed = centered * scaling
    return (normed * gain_row + shift_row, normed, scaling)


def normalize_back(incoming, normed, scaling, gain_row):
    scaled = incoming * gain_row
    first_sum, second_sum = lax.psum((jnp.sum(scaled, -1), jnp.sum(scaled * normed, -1)), "col")
    return scaling * (scaled - first_sum[:, None] / D - normed * second_sum[:, None] / D)


def attend_forward(inputs):
    queries, keys, values = inputs
    scores = jnp.einsum(
        "qhe,khe->hqk", queries, keys, preferred_element_type=jnp.float32
    ) * HEAD_DIM ** (-0.5)
    highest = jnp.max(scores, -1, keepdims=True)
    exponent = jnp.exp(scores - highest)
    totals = jnp.sum(exponent, -1, keepdims=True)
    context = jnp.einsum(
        "hqk,khe->qhe",
        (exponent / totals).astype(jnp.bfloat16),
        values,
        preferred_element_type=jnp.float32,
    )
    return (context, (highest + jnp.log(totals))[..., 0])


def attend_back(inputs):
    queries, keys, values, log_total, grad_context = inputs
    scaling = HEAD_DIM ** (-0.5)
    scores = jnp.einsum("qhe,khe->hqk", queries, keys, preferred_element_type=jnp.float32) * scaling
    probability = jnp.exp(scores - log_total[..., None])
    grad_prob = jnp.einsum("qhe,khe->hqk", grad_context, values, preferred_element_type=jnp.float32)
    row_dot = jnp.sum(probability * grad_prob, -1, keepdims=True)
    grad_score = (probability * (grad_prob - row_dot)).astype(jnp.bfloat16)
    grad_queries = (
        jnp.einsum("hqk,khe->qhe", grad_score, keys, preferred_element_type=jnp.float32) * scaling
    )
    grad_keys = (
        jnp.einsum("hqk,qhe->khe", grad_score, queries, preferred_element_type=jnp.float32)
        * scaling
    )
    grad_values = jnp.einsum(
        "hqk,qhe->khe",
        probability.astype(jnp.bfloat16),
        grad_context,
        preferred_element_type=jnp.float32,
    )
    return (
        grad_queries.astype(jnp.bfloat16),
        grad_keys.astype(jnp.bfloat16),
        grad_values.astype(jnp.bfloat16),
    )


def alternate(gradient, axis_dim, row_count, data_count):
    dims_now = gradient.shape
    block_size = dims_now[axis_dim] // (row_count * data_count)
    reshaped = gradient.reshape(
        dims_now[:axis_dim] + (row_count, data_count, block_size) + dims_now[axis_dim + 1 :]
    )
    return jnp.swapaxes(reshaped, axis_dim, axis_dim + 1).reshape(dims_now)


def adam_step(weight, mean_old, square_old, gradient, step_rate, decay_rate):
    mean_new = BETA_ONE * mean_old + (1.0 - BETA_ONE) * gradient
    square_new = BETA_TWO * square_old + (1.0 - BETA_TWO) * gradient * gradient
    mean_hat = mean_new / (1.0 - BETA_ONE**STEP)
    square_hat = square_new / (1.0 - BETA_TWO**STEP)
    weight_new = weight - step_rate * (
        mean_hat / (jnp.sqrt(square_hat) + ADAM_EPS) + decay_rate * weight
    )
    return (weight_new, mean_new, square_new)


def body(
    tokens,
    cotangent,
    qkv_weight,
    proj_weight,
    up_weight,
    down_weight,
    vectors,
    qkv_mean,
    qkv_square,
    proj_mean,
    proj_square,
    up_mean,
    up_square,
    down_mean,
    down_square,
    vector_mean,
    vector_square,
):
    heads_here = qkv_weight.shape[2] // HEAD_DIM
    tok_rows = tokens.shape[0]
    seq_count = tok_rows // SEQ
    head_shape = (seq_count, SEQ, heads_here, HEAD_DIM)
    qkv_full, proj_full, up_full, down_full = (
        lax.all_gather(qkv_weight.astype(jnp.bfloat16), "row", axis=1, tiled=True),
        lax.all_gather(proj_weight.astype(jnp.bfloat16), "row", axis=1, tiled=True),
        lax.all_gather(up_weight.astype(jnp.bfloat16), "row", axis=0, tiled=True),
        lax.all_gather(down_weight.astype(jnp.bfloat16), "row", axis=1, tiled=True),
    )
    query_bias = vectors[0]
    value_bias = vectors[1]
    proj_bias = vectors[2]
    down_bias = vectors[3]
    gain_first = vectors[4]
    shift_first = vectors[5]
    gain_second = vectors[6]
    shift_second = vectors[7]
    up_bias = vectors[8:12].reshape(-1)
    inputs_full = gather_features(tokens)
    queries = (matmul(inputs_full, qkv_full[0]) + query_bias).astype(jnp.bfloat16)
    keys = matmul(inputs_full, qkv_full[1]).astype(jnp.bfloat16)
    values = (matmul(inputs_full, qkv_full[2]) + value_bias).astype(jnp.bfloat16)
    query_heads = queries.reshape(head_shape)
    key_heads = keys.reshape(head_shape)
    value_heads = values.reshape(head_shape)
    context, log_total = lax.map(attend_forward, (query_heads, key_heads, value_heads))
    context = context.reshape(tok_rows, -1).astype(jnp.bfloat16)
    first_sum = tokens.astype(jnp.float32) + sum_partial(matmul(context, proj_full)) + proj_bias
    hidden_first, normed_first, scale_first = normalize(first_sum, gain_first, shift_first)
    hidden_full = gather_features(hidden_first.astype(jnp.bfloat16))
    pre_act = matmul(hidden_full, up_full) + up_bias
    activated = jax.nn.gelu(pre_act, approximate=False).astype(jnp.bfloat16)
    second_sum = hidden_first + sum_partial(matmul(activated, down_full)) + down_bias
    output, normed_second, scale_second = normalize(second_sum, gain_second, shift_second)
    grad_output = cotangent.astype(jnp.float32)
    grad_second = normalize_back(grad_output, normed_second, scale_second, gain_second)
    grad_gain_second = jnp.sum(grad_output * normed_second, 0)
    grad_shift_second = jnp.sum(grad_output, 0)
    grad_down_bias = jnp.sum(grad_second, 0)
    grad_branch = gather_grads(grad_second.astype(jnp.bfloat16))
    grad_down = left_contract(activated, grad_branch)
    grad_act = right_contract(grad_branch, down_full)
    gelu_pull = jax.vjp(partial(jax.nn.gelu, approximate=False), pre_act)[1]
    grad_pre = gelu_pull(grad_act)[0].astype(jnp.bfloat16)
    grad_up_bias = jnp.sum(grad_pre, 0, dtype=jnp.float32)
    grad_up = left_contract(hidden_full, grad_pre)
    grad_hidden = grad_second + sum_grad_partial(right_contract(grad_pre, up_full))
    grad_first = normalize_back(grad_hidden, normed_first, scale_first, gain_first)
    grad_gain_first = jnp.sum(grad_hidden * normed_first, 0)
    grad_shift_first = jnp.sum(grad_hidden, 0)
    grad_proj_bias = jnp.sum(grad_first, 0)
    grad_attn = gather_grads(grad_first.astype(jnp.bfloat16))
    grad_proj = left_contract(context, grad_attn)
    grad_context = right_contract(grad_attn, proj_full).astype(jnp.bfloat16)
    grad_queries, grad_keys, grad_values = lax.map(
        attend_back,
        (query_heads, key_heads, value_heads, log_total, grad_context.reshape(head_shape)),
    )
    grad_queries = grad_queries.reshape(tok_rows, -1)
    grad_keys = grad_keys.reshape(tok_rows, -1)
    grad_values = grad_values.reshape(tok_rows, -1)
    grad_qkv = jnp.stack(
        [
            left_contract(inputs_full, grad_queries),
            left_contract(inputs_full, grad_keys),
            left_contract(inputs_full, grad_values),
        ]
    )
    grad_inputs = (
        right_contract(grad_queries, qkv_full[0])
        + right_contract(grad_keys, qkv_full[1])
        + right_contract(grad_values, qkv_full[2])
    )
    input_grad = grad_first + sum_grad_partial(grad_inputs)
    grad_query_bias = jnp.sum(grad_queries, 0, dtype=jnp.float32)
    grad_value_bias = jnp.sum(grad_values, 0, dtype=jnp.float32)
    vector_grad = jnp.concatenate(
        [
            jnp.stack(
                [
                    grad_query_bias,
                    grad_value_bias,
                    grad_proj_bias,
                    grad_down_bias,
                    grad_gain_first,
                    grad_shift_first,
                    grad_gain_second,
                    grad_shift_second,
                ]
            ),
            grad_up_bias.reshape(4, -1),
        ],
        0,
    )
    vector_grad = lax.psum(vector_grad, ("dp", "row"))
    row_count = lax.axis_size("row")
    data_count = lax.axis_size("dp")
    pieces = (
        lax.psum_scatter(
            alternate(grad_qkv, 1, row_count, data_count),
            ("dp", "row"),
            scatter_dimension=1,
            tiled=True,
        ),
        lax.psum_scatter(
            alternate(grad_proj, 1, row_count, data_count),
            ("dp", "row"),
            scatter_dimension=1,
            tiled=True,
        ),
        lax.psum_scatter(
            alternate(grad_up, 0, row_count, data_count),
            ("dp", "row"),
            scatter_dimension=0,
            tiled=True,
        ),
        lax.psum_scatter(
            alternate(grad_down, 1, row_count, data_count),
            ("dp", "row"),
            scatter_dimension=1,
            tiled=True,
        ),
    )
    reduced = (
        lax.all_gather(pieces[0], "dp", axis=1, tiled=True),
        lax.all_gather(pieces[1], "dp", axis=1, tiled=True),
        lax.all_gather(pieces[2], "dp", axis=0, tiled=True),
        lax.all_gather(pieces[3], "dp", axis=1, tiled=True),
    )
    qkv_out = adam_step(qkv_weight, qkv_mean, qkv_square, reduced[0], RATE_QKV, DECAY_RATE)
    proj_out = adam_step(proj_weight, proj_mean, proj_square, reduced[1], RATE_PROJ, DECAY_RATE)
    up_out = adam_step(up_weight, up_mean, up_square, reduced[2], RATE_UP, DECAY_RATE)
    down_out = adam_step(down_weight, down_mean, down_square, reduced[3], RATE_DOWN, DECAY_RATE)
    vector_out = adam_step(vectors, vector_mean, vector_square, vector_grad, RATE_VECTOR, 0.0)
    return (
        output.astype(jnp.bfloat16),
        input_grad,
        qkv_out[0],
        qkv_out[1],
        qkv_out[2],
        proj_out[0],
        proj_out[1],
        proj_out[2],
        up_out[0],
        up_out[1],
        up_out[2],
        down_out[0],
        down_out[1],
        down_out[2],
        vector_out[0],
        vector_out[1],
        vector_out[2],
        vector_grad,
    )


def solution(mesh):
    return jax.shard_map(
        body,
        mesh=mesh,
        in_specs=(
            P(("dp", "row"), "col"),
            P(("dp", "row"), "col"),
            P(None, "row", "col"),
            P("col", "row"),
            P("row", "col"),
            P("col", "row"),
            P(None, "col"),
            P(None, "row", "col"),
            P(None, "row", "col"),
            P("col", "row"),
            P("col", "row"),
            P("row", "col"),
            P("row", "col"),
            P("col", "row"),
            P("col", "row"),
            P(None, "col"),
            P(None, "col"),
        ),
        out_specs=(
            P(("dp", "row"), "col"),
            P(("dp", "row"), "col"),
            P(None, "row", "col"),
            P(None, "row", "col"),
            P(None, "row", "col"),
            P("col", "row"),
            P("col", "row"),
            P("col", "row"),
            P("row", "col"),
            P("row", "col"),
            P("row", "col"),
            P("col", "row"),
            P("col", "row"),
            P("col", "row"),
            P(None, "col"),
            P(None, "col"),
            P(None, "col"),
            P(None, "col"),
        ),
        check_vma=False,
    )
```

profile of v0, /device:TPU:0, one launch (start us, length us, event | category | flops | bytes accessed | tf_op | source)
XLA Modules:
  0.0 552.6 jit_solution(783560227516751597)
XLA Ops:
  10.8 11.1 %all_gather.38 = bf16[256,512]{1,0:T(8,128)(2,1)} all-gather(bf16[256,128]{1,0:T(8,128)(2,1)S(1)} %convert_element_type.100), channel_id=1, replica_groups=mesh['dp'=4,'row'=4,'col'=2] {'row'}, dimensions={1}, use_global_device_ids=true | all-gather | bytes 327680 | tf_op jit(solution)/shard_map/all_gather | solution.py:163
  21.9 12.0 %all_gather.37 = bf16[3,512,256]{2,1,0:T(8,128)(2,1)S(1)} all-gather(bf16[3,128,256]{2,1,0:T(8,128)(2,1)S(1)} %convert_element_type.94), channel_id=1, replica_groups=mesh['dp'=4,'row'=4,'col'=2] {'row'}, dimensions={1}, use_global_device_ids=true | all-gather | bytes 983040 | tf_op jit(solution)/shard_map/all_gather | solution.py:162
  42.8 6.6 %while.26 = (s32[]{:T(128)}, bf16[2,512,4,64]{1,3,2,0:T(8,128)(2,1)}, f32[2,4,512]{2,1,0:T(4,128)S(1)}, bf16[2,512,4,64]{1,3,2,0:T(8,128)(2,1)S(1)}, bf16[2,512,...) while((s32[]{:T(128)}, bf16[2,512,4,64]{1,3,2,0:T(8,128)(2,1)}, ...), condition=%wide.region_3.4_spmd, body=%wide.region_0.3_spmd.sunk | while | flops 277870592 | bytes 18155656 | solution.py:183
  54.9 9.1 %reduce-scatter.9.cloned.1.call-done = f32[1024,256]{1,0:T(8,128)} async-done(((f32[1024,512]{1,0:T(8,128)}), f32[1024,256]{1,0:T(8,128)}) %reduce-scatter.9.cloned.1.call-update) | async-done | bytes 1048592 | tf_op jit(solution)/shard_map/reduce_scatter | solution.py:51
  73.0 10.6 %all-gather.11.cloned.1.call-done = bf16[512,1024]{1,0:T(8,128)(2,1)} async-done(((bf16[128,1024]{1,0:T(8,128)(2,1)}), bf16[512,1024]{1,0:T(8,128)(2,1)}) %all-gather.11.cloned.1.call-update) | async-done | bytes 1048592 | tf_op jit(solution)/shard_map/all_gather | solution.py:164
  83.6 11.0 %all-gather.9.cloned.1.call-done = bf16[1024,512]{1,0:T(8,128)(2,1)} async-done(((bf16[1024,256]{1,0:T(8,128)(2,1)}), bf16[1024,512]{1,0:T(8,128)(2,1)}) %all-gather.9.cloned.1.call-update) | async-done | bytes 1048592 | tf_op jit(solution)/shard_map/all_gather | solution.py:43
  94.6 13.2 %multiply_convert_fusion.1 = (bf16[1024,1024]{1,0:T(8,128)(2,1)}, f32[1024,1024]{1,0:T(8,128)}, f32[1024,1024]{1,0:T(8,128)}) fusion(f32[1024]{0:T(1024)S(1)} %bitcast.245, bf16[1024,512]{1,0:T(8,128)(2,1)} %all-gather.9.cloned.1.call-done, bf16[512,1024]{1,0:T(8,128)(2,1)} %all-gather.11.cloned.1.call-done), kind=kOutput, calls=%fused_computation.63 | convolution fusion | flops 1142947840 | bytes 12587008 | tf_op jit(solution)/shard_map/dot_general | solution.py:27
  107.7 16.8 %all-gather.13.cloned.1.call-done = bf16[1024,512]{1,0:T(8,128)(2,1)} async-done(((bf16[1024,128]{1,0:T(8,128)(2,1)}), bf16[1024,512]{1,0:T(8,128)(2,1)}) %all-gather.13.cloned.1.call-update) | async-done | bytes 1048592 | tf_op jit(solution)/shard_map/all_gather | solution.py:165
  124.6 4.4 fusion.93
  129.0 9.6 %reduce-scatter.11.cloned.1.call-done = f32[1024,256]{1,0:T(8,128)} async-done(((f32[1024,512]{1,0:T(8,128)}), f32[1024,256]{1,0:T(8,128)}) %reduce-scatter.11.cloned.1.call-update) | async-done | bytes 1048592 | tf_op jit(solution)/shard_map/reduce_scatter | solution.py:51
  150.5 3.0 fusion.81
  155.4 10.3 %all-gather.15.cloned.1.call-done = bf16[1024,512]{1,0:T(8,128)(2,1)} async-done(((bf16[1024,256]{1,0:T(8,128)(2,1)}), bf16[1024,512]{1,0:T(8,128)(2,1)}) %all-gather.15.cloned.1.call-update) | async-done | bytes 1048592 | tf_op jit(solution)/shard_map/all_gather | solution.py:47
  165.7 7.3 %convert_reduce_fusion = (f32[1024]{0:T(1024)}, bf16[1024,1024]{1,0:T(8,128)(2,1)S(1)}) fusion(f32[1024,1024]{1,0:T(8,128)} %get-tuple-element.251, bf16[1024,512]{1,0:T(8,128)(2,1)} %all-gather.15.cloned.1.call-done, bf16[1024,512]{1,0:T(8,128)(2,1)} %all-gather.13.cloned.1.call-done, f32[1024,1024]{1,0:T(8,128)} %get-tuple-element.267, f32[1024]{0:T(1024)S(1)} %bitcast.246), kind=kOutput, calls=%fused_computation.61 | convolution fusion | flops 1091566592 | bytes 12591104 | tf_op jit(solution)/shard_map/dot_general | solution.py:37
  176.9 10.9 %reduce-scatter.13.cloned.1.call-done = f32[1024,256]{1,0:T(8,128)} async-done(((f32[1024,512]{1,0:T(8,128)}), f32[1024,256]{1,0:T(8,128)}) %reduce-scatter.13.cloned.1.call-update) | async-done | bytes 1048592 | tf_op jit(solution)/shard_map/reduce_scatter | solution.py:55
  187.8 3.1 multiply_reduce_fusion.2
  214.8 13.5 %while.27 = (s32[]{:T(128)}, bf16[2,512,4,64]{1,3,2,0:T(8,128)(2,1)}, bf16[2,512,4,64]{1,3,2,0:T(8,128)(2,1)}, bf16[2,512,4,64]{1,3,2,0:T(8,128)(2,1)}, bf16[2,5...) while((s32[]{:T(128)}, ...), condition=%wide.region_25.26_spmd, body=%wide.region_23.25_spmd.sunk | while | flops 684324864 | bytes 42530008 | solution.py:212
  245.6 47.0 %reduce-scatter.23.cloned.1.call-done = f32[1024,32]{0,1:T(8,128)} async-done(((f32[1024,512]{0,1:T(8,128)}), f32[1024,32]{0,1:T(8,128)}) %reduce-scatter.23.cloned.1.call-update) | async-done | bytes 131088 | tf_op jit(solution)/shard_map/reduce_scatter | solution.py:274
  292.6 15.9 %all_gather.47 = f32[1024,128]{0,1:T(8,128)S(1)} all-gather(f32[1024,32]{0,1:T(8,128)} %reduce-scatter.23.cloned.1.call-done), channel_id=1, replica_groups=mesh['dp'=4,'row'=4,'col'=2] {'dp'}, dimensions={1}, use_global_device_ids=true | all-gather | bytes 655360 | tf_op jit(solution)/shard_map/all_gather | solution.py:285
  313.8 58.8 %reduce-scatter.21.cloned.1.call-done = f32[32,1024]{1,0:T(8,128)} async-done(((f32[512,1024]{1,0:T(8,128)}), f32[32,1024]{1,0:T(8,128)}) %reduce-scatter.21.cloned.1.call-update) | async-done | bytes 131088 | tf_op jit(solution)/shard_map/reduce_scatter | solution.py:268
  372.6 15.2 %all_gather.46 = f32[128,1024]{1,0:T(8,128)S(1)} all-gather(f32[32,1024]{1,0:T(8,128)} %reduce-scatter.21.cloned.1.call-done), channel_id=1, replica_groups=mesh['dp'=4,'row'=4,'col'=2] {'dp'}, dimensions={0}, use_global_device_ids=true | all-gather | bytes 655360 | tf_op jit(solution)/shard_map/all_gather | solution.py:284
  393.4 72.4 %psum.71 = f32[12,256]{1,0:T(8,128)S(1)} all-reduce(f32[12,256]{1,0:T(8,128)S(1)} %concatenate.4), channel_id=1, replica_groups=mesh['dp'=4,'row'=4,'col'=2] {'dp','row'}, use_global_device_ids=true, to_apply=%region_40.41 | all-reduce | flops 3072 | bytes 24576 | tf_op jit(solution)/shard_map/psum | solution.py:252
  467.2 13.7 %all_gather.45 = f32[256,128]{0,1:T(8,128)S(1)} all-gather(f32[256,32]{0,1:T(8,128)} %reduce-scatter.19.cloned.1.call-done), channel_id=1, replica_groups=mesh['dp'=4,'row'=4,'col'=2] {'dp'}, dimensions={1}, use_global_device_ids=true | all-gather | bytes 163840 | tf_op jit(solution)/shard_map/all_gather | solution.py:283
  483.3 42.5 %reduce-scatter.17.cloned.1.call-done = f32[3,32,256]{2,1,0:T(8,128)} async-done(((f32[3,512,256]{2,1,0:T(8,128)}), f32[3,32,256]{2,1,0:T(8,128)}) %reduce-scatter.17.cloned.1.call-update) | async-done | bytes 98320 | tf_op jit(solution)/shard_map/reduce_scatter | solution.py:256
  525.8 14.6 %all_gather.44 = f32[3,128,256]{2,1,0:T(8,128)S(1)} all-gather(f32[3,32,256]{2,1,0:T(8,128)} %reduce-scatter.17.cloned.1.call-done), channel_id=1, replica_groups=mesh['dp'=4,'row'=4,'col'=2] {'dp'}, dimensions={1}, use_global_device_ids=true | all-gather | bytes 491520 | tf_op jit(solution)/shard_map/all_gather | solution.py:282
  (238 shorter events, 123.5 us)
Async XLA Ops:
  8.0 27.0 %all-gather.7.cloned.1.call-start = ((), (), s32[]{:S(2)}) async-start(), calls=%async_computation.8 | async-start | bytes 1572864 | tf_op jit(solution)/shard_map/all_gather | solution.py:43
  8.8 55.2 %reduce-scatter.9.cloned.1.call-start = ((), (), s32[]{:S(2)}) async-start(), calls=%async_computation.9 | async-start | bytes 3145728 | tf_op jit(solution)/shard_map/reduce_scatter | solution.py:51
  49.4 14.6 %copy-start.6 = (bf16[2,512,4,64]{1,3,2,0:T(8,128)(2,1)}, bf16[2,512,4,64]{1,3,2,0:T(8,128)(2,1)S(1)}, u32[]{:S(2)}) copy-start(bf16[2,512,4,64]{1,3,2,0:T(8,128)(2,1)S(1)} %get-tuple-element.448) | copy-start | bytes 1572868
  49.4 14.6 %copy-start.12 = (bf16[1024,256]{1,0:T(8,128)(2,1)S(1)}, bf16[1024,256]{1,0:T(8,128)(2,1)}, u32[]{:S(2)}) copy-start(bf16[1024,256]{1,0:T(8,128)(2,1)} %param.21) | copy-start | bytes 1572868
  53.9 18.1 %copy-start.17 = (f32[1024,128]{1,0:T(8,128)S(1)}, f32[1024,128]{1,0:T(8,128)}, u32[]{:S(2)}) copy-start(f32[1024,128]{1,0:T(8,128)} %param.26) | copy-start | bytes 1572868
  54.0 19.0 %copy-start.34 = (f32[12,256]{1,0:T(8,128)S(1)}, f32[12,256]{1,0:T(8,128)}, u32[]{:S(2)}) copy-start(f32[12,256]{1,0:T(8,128)} %param.27) | copy-start | bytes 36868
  54.0 29.6 %all-gather.11.cloned.1.call-start = ((), (), s32[]{:S(2)}) async-start(), calls=%async_computation.11 | async-start | bytes 1310720 | tf_op jit(solution)/shard_map/all_gather | solution.py:164
  54.8 39.8 %all-gather.9.cloned.1.call-start = ((), (), s32[]{:S(2)}) async-start(), calls=%async_computation.10 | async-start | bytes 1572864 | tf_op jit(solution)/shard_map/all_gather | solution.py:43
  72.0 52.6 %all-gather.13.cloned.1.call-start = ((), (), s32[]{:S(2)}) async-start(), calls=%async_computation.12 | async-start | bytes 1310720 | tf_op jit(solution)/shard_map/all_gather | solution.py:165
  72.8 65.9 %reduce-scatter.11.cloned.1.call-start = ((), (), s32[]{:S(2)}) async-start(), calls=%async_computation.13 | async-start | bytes 3145728 | tf_op jit(solution)/shard_map/reduce_scatter | solution.py:51
  129.0 36.7 %all-gather.15.cloned.1.call-start = ((), (), s32[]{:S(2)}) async-start(), calls=%async_computation.14 | async-start | bytes 1572864 | tf_op jit(solution)/shard_map/all_gather | solution.py:47
  155.3 32.5 %reduce-scatter.13.cloned.1.call-start = ((), (), s32[]{:S(2)}) async-start(), calls=%async_computation.15 | async-start | bytes 3145728 | tf_op jit(solution)/shard_map/reduce_scatter | solution.py:55
  176.9 31.1 %all-gather.17.cloned.1.call-start = ((), (), s32[]{:S(2)}) async-start(), calls=%async_computation.16 | async-start | bytes 1572864 | tf_op jit(solution)/shard_map/all_gather | solution.py:47
  197.8 94.8 %reduce-scatter.23.cloned.1.call-start = ((), (), s32[]{:S(2)}) async-start(), calls=%async_computation.21 | async-start | bytes 2228224 | tf_op jit(solution)/shard_map/reduce_scatter | solution.py:274
  202.5 170.1 %reduce-scatter.21.cloned.1.call-start = ((), (), s32[]{:S(2)}) async-start(), calls=%async_computation.20 | async-start | bytes 2228224 | tf_op jit(solution)/shard_map/reduce_scatter | solution.py:268
  207.3 259.9 %reduce-scatter.19.cloned.1.call-start = ((), (), s32[]{:S(2)}) async-start(), calls=%async_computation.19 | async-start | bytes 557056 | tf_op jit(solution)/shard_map/reduce_scatter | solution.py:262
  214.7 311.1 %reduce-scatter.17.cloned.1.call-start = ((), (), s32[]{:S(2)}) async-start(), calls=%async_computation.18 | async-start | bytes 1671168 | tf_op jit(solution)/shard_map/reduce_scatter | solution.py:256
  214.8 15.2 %copy-start.1 = (bf16[1024,512]{1,0:T(8,128)(2,1)S(1)}, bf16[1024,512]{1,0:T(8,128)(2,1)}, u32[]{:S(2)}) copy-start(bf16[1024,512]{1,0:T(8,128)(2,1)} %all-gather.7.cloned.1.call-done) | copy-start | bytes 3145732
  240.3 302.4 %reduce-scatter.15.cloned.1.call-start = ((), (), s32[]{:S(2)}) async-start(), calls=%async_computation.17 | async-start | bytes 3145728 | tf_op jit(solution)/shard_map/reduce_scatter | solution.py:55
  244.9 142.9 %copy-start.14 = (f32[128,1024]{1,0:T(8,128)S(1)}, f32[128,1024]{1,0:T(8,128)}, u32[]{:S(2)}) copy-start(f32[128,1024]{1,0:T(8,128)} %param.25) | copy-start | bytes 1572868
  309.7 80.8 %copy-start.21 = (bf16[2,512,4,64]{1,3,2,0:T(8,128)(2,1)S(1)}, bf16[2,512,4,64]{1,3,2,0:T(8,128)(2,1)}, u32[]{:S(2)}) copy-start(bf16[2,512,4,64]{1,3,2,0:T(8,128)(2,1)} %get-tuple-element.102) | copy-start | bytes 1572868
  313.7 226.7 %copy-start.22 = (f32[3,128,256]{2,1,0:T(8,128)S(1)}, f32[3,128,256]{2,1,0:T(8,128)}, u32[]{:S(2)}) copy-start(f32[3,128,256]{2,1,0:T(8,128)} %param.23) | copy-start | bytes 1179652
  387.8 155.0 %copy-start.3 = (f32[1024,256]{1,0:T(8,128)S(1)}, f32[1024,256]{1,0:T(8,128)}, u32[]{:S(2)}) copy-start(f32[1024,256]{1,0:T(8,128)} %copy-done.2) | copy-start | bytes 3145732
  465.8 79.2 %copy-start.33 = (f32[12,256]{1,0:T(8,128)}, f32[12,256]{1,0:T(8,128)S(1)}, u32[]{:S(2)}) copy-start(f32[12,256]{1,0:T(8,128)S(1)} %psum.71) | copy-start | bytes 36868
  (34 other events, 96.5 us)
Sparse Core Ops, SparseCore 0:
  10.4 11.6 all-gather.6
  54.1 9.8 reduce-scatter.8
  155.4 10.1 all-gather.14
  177.0 10.7 reduce-scatter.12
Sparse Core Ops, SparseCore 1:
  56.9 26.7 all-gather.10
  85.7 8.8 all-gather.8
  97.0 27.5 all-gather.12
  129.1 9.5 reduce-scatter.10
  197.9 10.0 all-gather.16
  210.4 82.1 reduce-scatter.22
  294.8 77.7 reduce-scatter.20
  374.8 73.0 reduce-scatter.18
  450.0 75.8 reduce-scatter.16
  528.2 6.1 reduce-scatter.14
where the time goes:
time: 560 us; the launch traced here: 553 us
  waiting for transfers between devices  228 us (41%)
  blocking collectives  170 us (30%)
  matrix products  58.2 us (10%)
  local copies, waits for them, and re-layouts  40.9 us (7%)
  other arithmetic  37.6 us (7%)
  between operations  16.4 us (3%)
    psum x1, blocking collectives, body(): vector_grad = lax.psum(vector_grad, ('dp', 'row'))  72.4 us
    reduce_scatter x1, waiting for transfers between devices, body(): lax.psum_scatter(alternate(grad_up, 0, row_count, data_count), ('dp', 'ro...  58.8 us
    reduce_scatter x1, waiting for transfers between devices, body(): lax.psum_scatter(alternate(grad_down, 1, row_count, data_count), ('dp', '...  47 us
    reduce_scatter x1, waiting for transfers between devices, body(): lax.psum_scatter(alternate(grad_qkv, 1, row_count, data_count), ('dp', 'r...  42.5 us
    dot_general x6, matrix products, matmul(): return jnp.dot(left, right, preferred_element_type=jnp.float32)  22 us
    reduce_scatter x2, waiting for transfers between devices, sum_partial(): return lax.psum_scatter(summed, 'col', scatter_dimension=1, tiled=True)  18.8 us
    all_gather x1, waiting for transfers between devices, body(): lax.all_gather(down_weight.astype(jnp.bfloat16), 'row', axis=1, tiled=True)  16.8 us
    all_gather x1, blocking collectives, body(): lax.all_gather(pieces[3], 'dp', axis=1, tiled=True)  15.9 us
  transfers between devices with their start and end apart: 14, of which 11 were waited for; matrix products, arithmetic and copies ran while one was open for 15% of the time, Pallas kernels for 0%

commit v1 on v0

v1 whole, which is shorter than its diff:
```python
import functools

import jax
import jax.numpy as jnp
from jax import lax
from jax.experimental import pallas as pl
from jax.experimental.pallas import tpu as pltpu
from jax.sharding import PartitionSpec as P

MESH = pl.DeviceIdType.MESH
BF = jnp.bfloat16
F32 = jnp.float32

D = 512
HEADS = 8
HEAD_DIM = 64
FF = 2048
SEQ = 512
STEP = 10
ROWS = 4
HALF = D // 2
BLK = D // ROWS
HID = 512

NORM_EPS = 1e-05
BETA_ONE = 0.9
BETA_TWO = 0.999
ADAM_EPS = 1e-08
DECAY_RATE = 0.01
RATE_QKV = 0.03
RATE_PROJ = 0.3
RATE_UP = 0.03
RATE_DOWN = 0.02
RATE_VECTOR = 0.3
VMEM_BYTES = 60 * 2**20

GATHER_UNITS = ((0, 0), (0, 1), (0, 2), (1, 0), (2, 0), (3, 0), (2, 1), (3, 1))
REDUCE_UNITS = ((3, 0), (2, 0), (3, 1), (2, 1), (1, 0), (0, 0), (0, 1), (0, 2))


def at(start, size, multiple=128):
    return pl.ds(pl.multiple_of(start, multiple), size)


def mm(a, b):
    return jnp.dot(a, b, preferred_element_type=F32)


def mm_lt(a, b):
    return lax.dot_general(a, b, (((0,), (0,)), ((), ())), preferred_element_type=F32)


def mm_rt(a, b):
    return lax.dot_general(a, b, (((1,), (1,)), ((), ())), preferred_element_type=F32)


def piece(unit, full, r, c):
    kind, k = unit
    if kind == 0:
        return full[0].at[k, at(r * BLK, BLK), at(c * HALF, HALF)]
    if kind == 1:
        return full[1].at[at(c * HALF, HALF), at(r * BLK, BLK)]
    if kind == 2:
        return full[2].at[at(r * BLK, BLK), at(c * 2 * HID + k * HID, HID)]
    return full[3].at[at(c * 2 * HID + k * HID, HID), at(r * BLK, BLK)]


def own_piece(unit, own):
    kind, k = unit
    if kind == 0:
        return own[0].at[k]
    if kind == 1:
        return own[1]
    if kind == 2:
        return own[2].at[:, pl.ds(k * HID, HID)]
    return own[3].at[pl.ds(k * HID, HID), :]


def column(unit, full, c):
    kind, k = unit
    if kind == 0:
        return full[0].at[k, :, at(c * HALF, HALF)]
    if kind == 1:
        return full[1].at[at(c * HALF, HALF), :]
    if kind == 2:
        return full[2].at[:, at(c * 2 * HID + k * HID, HID)]
    return full[3].at[at(c * 2 * HID + k * HID, HID), :]


def column_shape(unit):
    return ((D, HALF), (HALF, D), (D, HID), (HID, D))[unit[0]]


def piece_shape(unit):
    return ((BLK, HALF), (HALF, BLK), (BLK, HID), (HID, BLK))[unit[0]]


def row_part(unit, col_ref, r):
    if unit[0] in (0, 2):
        return col_ref.at[at(r * BLK, BLK), :]
    return col_ref.at[:, at(r * BLK, BLK)]


def remote(src, dst, send, recv, **where):
    return pltpu.make_async_remote_copy(
        src_ref=src, dst_ref=dst, send_sem=send, recv_sem=recv, device_id=where, device_id_type=MESH
    )


def position():
    return lax.axis_index("row"), lax.axis_index("col")


def flip(r, bit):
    if bit == 1:
        return r + 1 - 2 * lax.rem(r, 2)
    if bit == 2:
        return lax.rem(r + 2, 4)
    return 3 - r


def greet(dp_count):
    r, c = position()
    barrier = pltpu.get_barrier_semaphore()
    peers = [{"col": 1 - c}, {"row": flip(r, 1)}, {"row": flip(r, 2)}]
    if dp_count:
        z = lax.axis_index("dp")
        peers += [{"dp": lax.rem(z + k, dp_count)} for k in range(1, dp_count)]
    for peer in peers:
        pl.semaphore_signal(barrier, inc=1, device_id=peer, device_id_type=MESH)
    pl.semaphore_wait(barrier, len(peers))


def gather_kernel(
    tok, cot, qkv, proj, up, down, vec,
    x_out, ct_out, qkv_out, proj_out, up_out, down_out, vec_out,
    own_qkv, own_proj, own_up, own_down, send, recv, send_in, recv_in,
):
    r, c = position()
    sib = 1 - c
    full = (qkv_out, proj_out, up_out, down_out)
    own = (own_qkv, own_proj, own_up, own_down)
    for src, dst in zip((qkv, proj, up, down), own):
        dst[...] = src[...].astype(BF)
    greet(0)
    started = []

    def go(copy):
        copy.start()
        started.append(copy)
        return copy

    ins = []
    for i, (src, dst) in enumerate(((tok, x_out), (cot, ct_out))):
        ins.append(go(remote(src.at[at(sib * SEQ, SEQ), :], dst.at[:, at(c * HALF, HALF)],
                             send_in.at[i], recv_in.at[i], col=sib)))
    ins.append(go(remote(vec, vec_out.at[c], send_in.at[2], recv_in.at[2], col=sib)))
    first = []
    for u, unit in enumerate(GATHER_UNITS):
        src, dst = own_piece(unit, own), piece(unit, full, r, c)
        first.append([
            go(remote(src, dst, send.at[u, 0], recv.at[u, 0], row=flip(r, 1))),
            go(remote(src, dst, send.at[u, 1], recv.at[u, 1], row=flip(r, 2))),
            go(remote(src, dst, send.at[u, 3], recv.at[u, 3], col=sib)),
        ])
    for src, dst in ((tok, x_out), (cot, ct_out)):
        dst[:, at(c * HALF, HALF)] = src[at(c * SEQ, SEQ), :]
    vec_out[c] = vec[...]
    for unit in GATHER_UNITS:
        piece(unit, full, r, c)[...] = own_piece(unit, own)[...]
    to_sib, across = [], []
    for u, unit in enumerate(GATHER_UNITS):
        for k, bit in ((0, 1), (1, 2)):
            first[u][k].wait_recv()
            block = piece(unit, full, flip(r, bit), c)
            if k == u % 2:
                across.append(go(remote(block, block, send.at[u, 2], recv.at[u, 2], row=flip(r, 3 - bit))))
            to_sib.append(go(remote(block, block, send.at[u, 4 + k], recv.at[u, 4 + k], col=sib)))
        if u >= 1:
            v = u - 1
            across[v].wait_recv()
            block = piece(GATHER_UNITS[v], full, flip(r, 3), c)
            to_sib.append(go(remote(block, block, send.at[v, 6], recv.at[v, 6], col=sib)))
    v = len(GATHER_UNITS) - 1
    across[v].wait_recv()
    block = piece(GATHER_UNITS[v], full, flip(r, 3), c)
    to_sib.append(go(remote(block, block, send.at[v, 6], recv.at[v, 6], col=sib)))
    for copy in ins:
        copy.wait_recv()
    for u in range(len(GATHER_UNITS)):
        first[u][2].wait_recv()
    for copy in to_sib:
        copy.wait_recv()
    for copy in started:
        copy.wait_send()


def norm_forward(total):
    mean = jnp.mean(total, -1, keepdims=True)
    centered = total - mean
    scale = lax.rsqrt(jnp.mean(centered * centered, -1, keepdims=True) + NORM_EPS)
    return centered * scale, scale


def norm_back(grad, normed, scale, gain):
    scaled = grad * gain
    return scale * (
        scaled - jnp.mean(scaled, -1, keepdims=True) - normed * jnp.mean(scaled * normed, -1, keepdims=True)
    )


def layer_kernel(
    x_ref, ct_ref, qkv, proj, up, down, vec,
    bo_ref, ig_ref, dqkv, dproj, dup, ddown, vg,
    q_s, k_s, v_s, p_s, a_s, u_s, gp_s, h1_s, n1_s, da_s, dq_s, dk_s, dv_s,
):
    def row(i):
        return jnp.concatenate([vec[0, i:i + 1, :], vec[1, i:i + 1, :]], 1)

    def put_row(i, value):
        vg[0, i:i + 1, :] = value[:, :HALF]
        vg[1, i:i + 1, :] = value[:, HALF:]

    def col_sum(value):
        return jnp.sum(value, 0, keepdims=True)

    x = x_ref[...]
    scaling = HEAD_DIM ** (-0.5)
    q_s[...] = (mm(x, qkv[0]) + row(0)).astype(BF)
    k_s[...] = mm(x, qkv[1]).astype(BF)
    v_s[...] = (mm(x, qkv[2]) + row(1)).astype(BF)
    for h in range(HEADS):
        cols = slice(h * HEAD_DIM, (h + 1) * HEAD_DIM)
        s = mm_rt(q_s[:, cols], k_s[:, cols]) * scaling
        e = jnp.exp(s - jnp.max(s, -1, keepdims=True))
        p = e * (1.0 / jnp.sum(e, -1, keepdims=True))
        p_s[h] = p
        a_s[:, cols] = mm(p.astype(BF), v_s[:, cols]).astype(BF)
    n1, scale1 = norm_forward(x.astype(F32) + mm(a_s[...], proj[...]) + row(2))
    n1_s[...] = n1
    h1 = n1 * row(4) + row(5)
    h1b = h1.astype(BF)
    h1_s[...] = h1b
    acc = h1 + row(3)
    for j in range(4):
        c, k = j // 2, 2 * (j % 2)
        bias = jnp.concatenate([vec[c, 8 + k:9 + k, :], vec[c, 9 + k:10 + k, :]], 1)
        cols = slice(j * HID, (j + 1) * HID)
        z = mm(h1b, up[:, cols]) + bias
        half = 0.5 + 0.5 * lax.erf(z * 0.7071067811865476)
        u = (z * half).astype(BF)
        u_s[:, cols] = u
        gp_s[:, cols] = half + z * (0.3989422804014327 * jnp.exp(-0.5 * z * z))
        acc = acc + mm(u, down[cols, :])
    n2, scale2 = norm_forward(acc)
    bo_ref[...] = (n2 * row(6) + row(7)).astype(BF)
    dy = ct_ref[...].astype(F32)
    put_row(6, col_sum(dy * n2))
    put_row(7, col_sum(dy))
    dr2 = norm_back(dy, n2, scale2, row(6))
    put_row(3, col_sum(dr2))
    g2 = dr2.astype(BF)
    acc = dr2
    for j in (0, 2, 1, 3):
        c, k = j // 2, 2 * (j % 2)
        cols = slice(j * HID, (j + 1) * HID)
        ddown[cols, :] = mm_lt(u_s[:, cols], g2).astype(BF)
        dz = (mm_rt(g2, down[cols, :]) * gp_s[:, cols]).astype(BF)
        db = col_sum(dz.astype(F32))
        vg[c, 8 + k:9 + k, :] = db[:, :HALF]
        vg[c, 9 + k:10 + k, :] = db[:, HALF:]
        dup[:, cols] = mm_lt(h1_s[...], dz).astype(BF)
        acc = acc + mm_rt(dz, up[:, cols])
    n1 = n1_s[...]
    put_row(4, col_sum(acc * n1))
    put_row(5, col_sum(acc))
    dr1 = norm_back(acc, n1, scale1, row(4))
    put_row(2, col_sum(dr1))
    ig_ref[...] = dr1
    g1 = dr1.astype(BF)
    dproj[...] = mm_lt(a_s[...], g1).astype(BF)
    da_s[...] = mm_rt(g1, proj[...]).astype(BF)
    for h in range(HEADS):
        cols = slice(h * HEAD_DIM, (h + 1) * HEAD_DIM)
        da = da_s[:, cols]
        p = p_s[h]
        dp = mm_rt(da, v_s[:, cols])
        ds = (p * (dp - jnp.sum(p * dp, -1, keepdims=True))).astype(BF)
        dq_s[:, cols] = (mm(ds, k_s[:, cols]) * scaling).astype(BF)
        dk_s[:, cols] = (mm_lt(ds, q_s[:, cols]) * scaling).astype(BF)
        dv_s[:, cols] = mm_lt(p.astype(BF), da).astype(BF)
    dq, dk, dv = dq_s[...], dk_s[...], dv_s[...]
    put_row(0, col_sum(dq.astype(F32)))
    put_row(1, col_sum(dv.astype(F32)))
    dqkv[0] = mm_lt(x, dq).astype(BF)
    dqkv[1] = mm_lt(x, dk).astype(BF)
    dqkv[2] = mm_lt(x, dv).astype(BF)
    ig_ref[...] = ig_ref[...] + mm_rt(dq, qkv[0]) + mm_rt(dk, qkv[1]) + mm_rt(dv, qkv[2])


def reduce_kernel(dp_count, *refs):
    n = len(REDUCE_UNITS)
    bo, ig, dqkv, dproj, dup, ddown, vg = refs[:7]
    bo_out, ig_out, gqkv, gproj, gup, gdown, gvec = refs[7:14]
    rest = list(refs[14:])
    sib_buf, sums, buf_a, buf_b, send_b, zsrc, zbuf = (
        [rest.pop(0) for _ in range(n)] for _ in range(7)
    )
    vsum, vbuf, send, recv, send_v, recv_v = rest
    full, outs = (dqkv, dproj, dup, ddown), (gqkv, gproj, gup, gdown)
    r, c = position()
    sib = 1 - c
    z = lax.axis_index("dp") if dp_count else None
    greet(dp_count)
    started = []

    def go(copy):
        copy.start()
        started.append(copy)
        return copy

    flying = {}

    def wait(key):
        for copy in flying.pop(key):
            copy.wait_recv()

    def add(*views):
        total = views[0][...].astype(F32)
        for view in views[1:]:
            total = total + view[...].astype(F32)
        return total

    def quarter(unit, ref, k):
        depth = piece_shape(unit)[0] // dp_count
        return ref.at[at(k * depth, depth, 16), :]

    def phase(u, step):
        unit = REDUCE_UNITS[u]
        a, b = (1, 2) if u % 2 == 0 else (2, 1)
        if step == 0:
            flying[u] = [go(remote(column(unit, full, sib), sib_buf[u], send.at[u, 0], recv.at[u, 0], col=sib))]
        elif step == 1:
            wait(u)
            sums[u][...] = add(column(unit, full, c), sib_buf[u]).astype(BF)
            peer = flip(r, a)
            flying[u] = [
                go(remote(row_part(unit, sums[u], who), buf_a[u].at[i], send.at[u, 1 + i], recv.at[u, 1 + i], row=peer))
                for i, who in ((1, flip(r, 3)), (0, peer))
            ]
        elif step == 2:
            wait(u)
            send_b[u][...] = add(row_part(unit, sums[u], flip(r, b)), buf_a[u].at[1]).astype(BF)
            flying[u] = [go(remote(send_b[u], buf_b[u], send.at[u, 3], recv.at[u, 3], row=flip(r, b)))]
        elif step == 3:
            wait(u)
            total = add(row_part(unit, sums[u], r), buf_a[u].at[0], buf_b[u]).astype(BF)
            if not dp_count:
                own_piece(unit, outs)[...] = total
                return
            zsrc[u][...] = total
            flying[u] = []
            for k in range(1, dp_count):
                to = lax.rem(z + k, dp_count)
                flying[u].append(go(remote(
                    quarter(unit, zsrc[u], to), zbuf[u].at[k - 1], send.at[u, 3 + k], recv.at[u, 3 + k], dp=to)))
        elif step == 4:
            if not dp_count:
                return
            wait(u)
            mine = quarter(unit, own_piece(unit, outs), z)
            mine[...] = add(quarter(unit, zsrc[u], z), *[zbuf[u].at[k] for k in range(dp_count - 1)]).astype(BF)
            flying[u] = []
            for k in range(1, dp_count):
                to = lax.rem(z + k, dp_count)
                flying[u].append(go(remote(
                    mine, mine, send.at[u, 2 + dp_count + k], recv.at[u, 2 + dp_count + k], dp=to)))
        else:
            if dp_count:
                wait(u)

    phase(0, 0)
    phase(1, 0)
    back = [
        go(remote(src.at[:, at(sib * HALF, HALF)], dst.at[at(c * SEQ, SEQ), :], send_v.at[i], recv_v.at[i], col=sib))
        for i, (src, dst) in enumerate(((bo, bo_out), (ig, ig_out)))
    ]
    for src, dst in ((bo, bo_out), (ig, ig_out)):
        dst[at(c * SEQ, SEQ), :] = src[:, at(c * HALF, HALF)]

    def vec_step(step):
        if step == 0:
            flying["v"] = [go(remote(vg.at[sib], vbuf.at[0], send_v.at[2], recv_v.at[2], col=sib))]
        elif step == 1:
            wait("v")
            vsum[0] = vg[c] + vbuf[0]
            flying["v"] = [go(remote(vsum.at[0], vbuf.at[1], send_v.at[3], recv_v.at[3], row=flip(r, 1)))]
        elif step == 2:
            wait("v")
            vsum[1] = vsum[0] + vbuf[1]
            flying["v"] = [go(remote(vsum.at[1], vbuf.at[2], send_v.at[4], recv_v.at[4], row=flip(r, 2)))]
        elif step == 3:
            wait("v")
            total = vsum[1] + vbuf[2]
            if not dp_count:
                gvec[...] = total
                return
            vsum[2] = total
            flying["v"] = [
                go(remote(vsum.at[2], vbuf.at[2 + k], send_v.at[4 + k], recv_v.at[4 + k],
                          dp=lax.rem(z + k, dp_count)))
                for k in range(1, dp_count)
            ]
        elif step == 4 and dp_count:
            wait("v")
            parts = [vsum[2]] + [vbuf[2 + k] for k in range(1, dp_count)]
            total = jnp.zeros_like(parts[0])
            for owner in range(dp_count):
                for k, part in enumerate(parts):
                    total = total + jnp.where(lax.rem(z + dp_count - k, dp_count) == owner, part, 0.0)
            gvec[...] = total

    for tick in range(1, n + 6):
        for step in (5, 4, 3, 2, 1):
            u = tick - step
            if 0 <= u < n:
                phase(u, step)
        if tick + 1 < n:
            phase(tick + 1, 0)
        if tick <= 5:
            vec_step(tick - 1)
    for copy in back:
        copy.wait_recv()
    for copy in started:
        copy.wait_send()


def adam_step(weight, mean_old, square_old, gradient, step_rate, decay_rate):
    mean_new = BETA_ONE * mean_old + (1.0 - BETA_ONE) * gradient
    square_new = BETA_TWO * square_old + (1.0 - BETA_TWO) * gradient * gradient
    mean_hat = mean_new / (1.0 - BETA_ONE**STEP)
    square_hat = square_new / (1.0 - BETA_TWO**STEP)
    weight_new = weight - step_rate * (
        mean_hat / (jnp.sqrt(square_hat) + ADAM_EPS) + decay_rate * weight
    )
    return (weight_new, mean_new, square_new)


def shape(dims, dtype):
    return jax.ShapeDtypeStruct(dims, dtype)


def call(kernel, ins, outs, scratch, collective_id=None):
    vmem = pl.BlockSpec(memory_space=pltpu.VMEM)
    extra = {} if collective_id is None else dict(collective_id=collective_id, has_side_effects=True)
    return pl.pallas_call(
        kernel,
        out_shape=outs,
        in_specs=[vmem] * len(ins),
        out_specs=[vmem] * len(outs),
        scratch_shapes=scratch,
        compiler_params=pltpu.CompilerParams(vmem_limit_bytes=VMEM_BYTES, **extra),
    )(*ins)


FULL = ((3, D, D), (D, D), (D, FF), (FF, D))
OWN = ((3, BLK, HALF), (HALF, BLK), (BLK, FF // 2), (FF // 2, BLK))


def body(
    dp_size,
    tokens, cotangent, qkv_weight, proj_weight, up_weight, down_weight, vectors,
    qkv_mean, qkv_square, proj_mean, proj_square, up_mean, up_square,
    down_mean, down_square, vector_mean, vector_square,
):
    dma = pltpu.SemaphoreType.DMA
    vm = pltpu.VMEM
    n = len(GATHER_UNITS)
    gathered = call(
        gather_kernel,
        (tokens, cotangent, qkv_weight, proj_weight, up_weight, down_weight, vectors),
        [shape((SEQ, D), BF)] * 2 + [shape(s, BF) for s in FULL] + [shape((2, 12, HALF), F32)],
        [vm(s, BF) for s in OWN] + [dma((n, 7)), dma((n, 7)), dma((3,)), dma((3,))],
        collective_id=0,
    )
    sq = vm((SEQ, D), BF)
    partial = call(
        layer_kernel,
        gathered,
        [shape((SEQ, D), BF), shape((SEQ, D), F32)] + [shape(s, BF) for s in FULL] + [shape((2, 12, HALF), F32)],
        [sq, sq, sq, vm((HEADS, SEQ, SEQ), F32), sq, vm((SEQ, FF), BF), vm((SEQ, FF), F32), sq,
         vm((SEQ, D), F32), sq, sq, sq, sq],
    )
    dp_count = dp_size if dp_size == 4 else 0
    zn = dp_count or 4
    units = REDUCE_UNITS
    pieces = [piece_shape(u) for u in units]
    reduced = call(
        functools.partial(reduce_kernel, dp_count),
        partial,
        [shape((2 * SEQ, HALF), BF), shape((2 * SEQ, HALF), F32)] + [shape(s, BF) for s in OWN]
        + [shape((12, HALF), F32)],
        [vm(column_shape(u), BF) for u in units] + [vm(column_shape(u), BF) for u in units]
        + [vm((2,) + s, BF) for s in pieces] + [vm(s, BF) for s in pieces] + [vm(s, BF) for s in pieces]
        + [vm(s, BF) for s in pieces] + [vm((zn - 1, s[0] // zn, s[1]), BF) for s in pieces]
        + [vm((3, 12, HALF), F32), vm((2 + zn, 12, HALF), F32),
           dma((n, 3 + 2 * zn)), dma((n, 3 + 2 * zn)), dma((4 + zn,)), dma((4 + zn,))],
        collective_id=1,
    )
    output, input_grad, grads, vector_grad = reduced[0], reduced[1], reduced[2:6], reduced[6]
    grads = [g.astype(F32) for g in grads]
    if not dp_count:
        grads = [lax.psum(g, "dp") for g in grads]
        vector_grad = lax.psum(vector_grad, "dp")
    return (
        output,
        input_grad,
        *adam_step(qkv_weight, qkv_mean, qkv_square, grads[0], RATE_QKV, DECAY_RATE),
        *adam_step(proj_weight, proj_mean, proj_square, grads[1], RATE_PROJ, DECAY_RATE),
        *adam_step(up_weight, up_mean, up_square, grads[2], RATE_UP, DECAY_RATE),
        *adam_step(down_weight, down_mean, down_square, grads[3], RATE_DOWN, DECAY_RATE),
        *adam_step(vectors, vector_mean, vector_square, vector_grad, RATE_VECTOR, 0.0),
        vector_grad,
    )


def solution(mesh):
    tokens = P(("dp", "row"), "col")
    qkv, proj, up, down, vec = P(None, "row", "col"), P("col", "row"), P("row", "col"), P("col", "row"), P(None, "col")
    return jax.shard_map(
        functools.partial(body, mesh.shape["dp"]),
        mesh=mesh,
        in_specs=(tokens, tokens, qkv, proj, up, down, vec, qkv, qkv, proj, proj, up, up, down, down, vec, vec),
        out_specs=(tokens, tokens) + (qkv,) * 3 + (proj,) * 3 + (up,) * 3 + (down,) * 3 + (vec,) * 4,
        check_vma=False,
    )
```

time: 560 us -> 164 us (0.29); the launches traced: 553 us -> 164 us
  waiting for transfers between devices: 228 us -> 0 us
  blocking collectives: 170 us -> 0 us
  Pallas kernels: 0 us -> 152 us
  matrix products: 58.2 us -> 0 us
  local copies, waits for them, and re-layouts: 40.9 us -> 2.97 us
  other arithmetic: 37.6 us -> 8.07 us
  between operations: 16.4 us -> 0.84 us
    reduce_scatter x8 -> x0, waiting for transfers between devices: 178 us -> none  [the longest x1 58.8 us: body(): lax.psum_scatter(alternate(grad_up, 0, row_count, data_count), ('dp', 'ro...]
    pallas_call x0 -> x3, Pallas kernels: none -> 152 us  [call(): pl.pallas_call(kernel, out_shape=outs, in_specs=[vmem] * len(ins), out_sp...]
    psum x7 -> x0, blocking collectives: 87.4 us -> none  [the longest x1 72.4 us: body(): vector_grad = lax.psum(vector_grad, ('dp', 'row'))]
    all_gather x6 -> x0, blocking collectives: 82.4 us -> none  [the longest x1 15.9 us: body(): lax.all_gather(pieces[3], 'dp', axis=1, tiled=True)]
    dot_general x32 -> x0, matrix products: 58.2 us -> none  [the longest x6 22 us: matmul(): return jnp.dot(left, right, preferred_element_type=jnp.float32)]
    all_gather x6 -> x0, waiting for transfers between devices: 49.4 us -> none  [the longest x1 16.8 us: body(): lax.all_gather(down_weight.astype(jnp.bfloat16), 'row', axis=1, tiled=True)]
    reduce_sum x11 -> x0, other arithmetic: 17.4 us -> none  [the longest x2 3.18 us: normalize(): mean_row = (lax.psum(jnp.sum(summed, -1), 'col') / D)[:, None]]
    while x31 -> x0, local copies, waits for them, and re-layouts: 10.4 us -> none  [the longest x4 4.4 us: body(): lax.map(attend_back, (query_heads, key_heads, value_heads, log_total, gra...]
  transfers between devices with their start and end apart: 14 -> 0, of which waited for: 11 -> 0; matrix products, arithmetic and copies ran while one was open for 15% -> 0% of each run, Pallas kernels for 0% -> 0%
where the time goes in v1:
time: 164 us
  Pallas kernels  152 us (93%)
  other arithmetic  8.07 us (5%)
  local copies, waits for them, and re-layouts  2.97 us (2%)
    pallas_call x3, Pallas kernels, call(): pl.pallas_call(kernel, out_shape=outs, in_specs=[vmem] * len(ins), out_sp...  152 us
    sub x5, other arithmetic, adam_step(): weight - step_rate * (mean_hat / (jnp.sqrt(square_hat) + ADAM_EPS) + deca...  8.07 us

profile of v1, /device:TPU:0, one launch (start us, length us, event | category | flops | bytes accessed | tf_op | source)
XLA Modules:
  0.0 163.8 jit_solution(2964528173449782386)
XLA Ops:
  0.7 41.9 %shard_map.304 = (bf16[512,512]{1,0:T(8,128)(2,1)}, bf16[512,512]{1,0:T(8,128)(2,1)}, bf16[3,512,512]{2,1,0:T(8,128)(2,1)}, bf16[512,512]{1,0:T(8,128)(2,1)}, bf...) custom-call(bf16[1024,256]{1,0:T(8,128)(2,1)} %tok.1, bf16[1024,256]{1,0:T(8,128)(2,1)} %cot.1, ...), custom_call_target="tpu_custom_call" | custom-call | tf_op jit(solution)/shard_map/pallas_call | solution.py:456
  42.6 28.7 %shard_map.305 = (bf16[512,512]{1,0:T(8,128)(2,1)}, f32[512,512]{1,0:T(8,128)}, bf16[3,512,512]{2,1,0:T(8,128)(2,1)}, bf16[512,512]{1,0:T(8,128)(2,1)}, bf16[512...) custom-call(bf16[512,512]{1,0:T(8,128)(2,1)} %get-tuple-element.39.x_ref, ...), custom_call_target="tpu_custom_call" | custom-call | tf_op jit(solution)/shard_map/pallas_call | solution.py:456
  71.3 0.0 copy-start.19
  71.3 0.0 copy-start.5
  71.3 0.0 copy-start.14
  71.4 0.0 copy-start.15
  71.4 0.0 copy-start.2
  71.4 0.0 copy-start.10
  71.4 0.0 copy-start.11
  71.4 81.3 %shard_map.306 = (bf16[1024,256]{1,0:T(8,128)(2,1)}, f32[1024,256]{1,0:T(8,128)}, bf16[3,128,256]{2,1,0:T(8,128)(2,1)}, bf16[256,128]{1,0:T(8,128)(2,1)}, bf16[1...) custom-call(bf16[512,512]{1,0:T(8,128)(2,1)} %get-tuple-element.46.refs_0_, ...), custom_call_target="tpu_custom_call" | custom-call | tf_op jit(solution)/shard_map/pallas_call | solution.py:456
  152.7 0.0 copy-start
  152.7 0.0 copy-start.6
  152.7 0.0 copy-start.7
  152.8 1.5 multiply_subtract_fusion.4
  154.3 0.0 copy-done.14
  154.3 1.6 %multiply_subtract_fusion.3 = (f32[256,128]{1,0:T(8,128)}, f32[256,128]{1,0:T(8,128)}, f32[256,128]{1,0:T(8,128)}) fusion(f32[256,128]{1,0:T(8,128)S(1)} %copy-done.5, bf16[256,128]{1,0:T(8,128)(2,1)} %get-tuple-element.56, f32[256,128]{1,0:T(8,128)S(1)} %copy-done.14, f32[256,128]{1,0:T(8,128)S(1)} %copy-done.15), kind=kLoop, calls=%fused_computation.19 | loop fusion | flops 524288 | bytes 851968 | tf_op jit(solution)/shard_map/sub | solution.py:443
  155.9 2.1 %multiply_subtract_fusion.2 = (f32[3,128,256]{2,1,0:T(8,128)}, f32[3,128,256]{2,1,0:T(8,128)}, f32[3,128,256]{2,1,0:T(8,128)}) fusion(f32[3,128,256]{2,1,0:T(8,128)S(1)} %copy-done.2, bf16[3,128,256]{2,1,0:T(8,128)(2,1)} %get-tuple-element.55, f32[3,128,256]{2,1,0:T(8,128)S(1)} %copy-done.10, f32[3,128,256]{2,1,0:T(8,128)S(1)} %copy-done.11), kind=kLoop, calls=%fused_computation.14 | loop fusion | flops 1572864 | bytes 2555904 | tf_op jit(solution)/shard_map/sub | solution.py:443
  158.1 1.4 multiply_subtract_fusion.1
  159.5 0.4 copy-done.9
  159.9 0.1 copy-done.12
  160.0 1.4 multiply_subtract_fusion
  161.4 0.8 copy.38
  162.2 1.0 copy.39
  163.2 0.6 copy.40
  (27 shorter events, 0.1 us)
Async XLA Ops:
  71.3 81.5 %copy-start.16 = (f32[12,256]{1,0:T(8,128)S(1)}, f32[12,256]{1,0:T(8,128)}, u32[]{:S(2)}) copy-start(f32[12,256]{1,0:T(8,128)} %vec.1) | copy-start | bytes 36868
  71.3 81.5 %copy-start.18 = (f32[12,256]{1,0:T(8,128)S(1)}, f32[12,256]{1,0:T(8,128)}, u32[]{:S(2)}) copy-start(f32[12,256]{1,0:T(8,128)} %param.32) | copy-start | bytes 36868
  71.3 81.5 %copy-start.19 = (f32[12,256]{1,0:T(8,128)S(1)}, f32[12,256]{1,0:T(8,128)}, u32[]{:S(2)}) copy-start(f32[12,256]{1,0:T(8,128)} %param.33) | copy-start | bytes 36868
  71.3 82.9 %copy-start.5 = (f32[256,128]{1,0:T(8,128)S(1)}, f32[256,128]{1,0:T(8,128)}, u32[]{:S(2)}) copy-start(f32[256,128]{1,0:T(8,128)} %proj.1) | copy-start | bytes 393220
  71.3 82.9 %copy-start.14 = (f32[256,128]{1,0:T(8,128)S(1)}, f32[256,128]{1,0:T(8,128)}, u32[]{:S(2)}) copy-start(f32[256,128]{1,0:T(8,128)} %param.26) | copy-start | bytes 393220
  71.4 82.9 %copy-start.15 = (f32[256,128]{1,0:T(8,128)S(1)}, f32[256,128]{1,0:T(8,128)}, u32[]{:S(2)}) copy-start(f32[256,128]{1,0:T(8,128)} %param.27) | copy-start | bytes 393220
  71.4 84.5 %copy-start.2 = (f32[3,128,256]{2,1,0:T(8,128)S(1)}, f32[3,128,256]{2,1,0:T(8,128)}, u32[]{:S(2)}) copy-start(f32[3,128,256]{2,1,0:T(8,128)} %qkv.1) | copy-start | bytes 1179652
  71.4 84.5 %copy-start.10 = (f32[3,128,256]{2,1,0:T(8,128)S(1)}, f32[3,128,256]{2,1,0:T(8,128)}, u32[]{:S(2)}) copy-start(f32[3,128,256]{2,1,0:T(8,128)} %param.24) | copy-start | bytes 1179652
  71.4 84.5 %copy-start.11 = (f32[3,128,256]{2,1,0:T(8,128)S(1)}, f32[3,128,256]{2,1,0:T(8,128)}, u32[]{:S(2)}) copy-start(f32[3,128,256]{2,1,0:T(8,128)} %param.25) | copy-start | bytes 1179652
  152.7 5.3 %copy-start = (f32[128,1024]{1,0:T(8,128)S(1)}, f32[128,1024]{1,0:T(8,128)}, u32[]{:S(2)}) copy-start(f32[128,1024]{1,0:T(8,128)} %up.1) | copy-start | bytes 1572868
  152.7 5.3 %copy-start.6 = (f32[128,1024]{1,0:T(8,128)S(1)}, f32[128,1024]{1,0:T(8,128)}, u32[]{:S(2)}) copy-start(f32[128,1024]{1,0:T(8,128)} %param.28) | copy-start | bytes 1572868
  152.7 5.3 %copy-start.7 = (f32[128,1024]{1,0:T(8,128)S(1)}, f32[128,1024]{1,0:T(8,128)}, u32[]{:S(2)}) copy-start(f32[128,1024]{1,0:T(8,128)} %param.29) | copy-start | bytes 1572868
  152.7 5.3 %copy-start.13 = (bf16[128,1024]{1,0:T(8,128)(2,1)S(1)}, bf16[128,1024]{1,0:T(8,128)(2,1)}, u32[]{:S(2)}) copy-start(bf16[128,1024]{1,0:T(8,128)(2,1)} %get-tuple-element.57) | copy-start | bytes 786436
  158.0 1.5 copy-start.1
  158.0 1.5 copy-start.8
  158.0 1.9 %copy-start.9 = (f32[1024,128]{1,0:T(8,128)S(1)}, f32[1024,128]{1,0:T(8,128)}, u32[]{:S(2)}) copy-start(f32[1024,128]{1,0:T(8,128)} %param.31) | copy-start | bytes 1572868
  158.0 2.0 %copy-start.12 = (bf16[1024,128]{1,0:T(8,128)(2,1)S(1)}, bf16[1024,128]{1,0:T(8,128)(2,1)}, u32[]{:S(2)}) copy-start(bf16[1024,128]{1,0:T(8,128)(2,1)} %get-tuple-element.58) | copy-start | bytes 786436
  159.5 1.9 %copy-start.4 = (bf16[1024,256]{1,0:T(8,128)(2,1)S(1)}, bf16[1024,256]{1,0:T(8,128)(2,1)}, u32[]{:S(2)}) copy-start(bf16[1024,256]{1,0:T(8,128)(2,1)} %get-tuple-element.93) | copy-start | bytes 1572868
  160.0 2.2 %copy-start.3 = (f32[1024,256]{1,0:T(8,128)S(1)}, f32[1024,256]{1,0:T(8,128)}, u32[]{:S(2)}) copy-start(f32[1024,256]{1,0:T(8,128)} %get-tuple-element.94) | copy-start | bytes 3145732
  161.4 1.8 %copy-start.17 = (f32[12,256]{1,0:T(8,128)S(1)}, f32[12,256]{1,0:T(8,128)}, u32[]{:S(2)}) copy-start(f32[12,256]{1,0:T(8,128)} %get-tuple-element.110) | copy-start | bytes 36868

commit v2 on v1

v2 whole, which is shorter than its diff:
```python
import functools

import jax
import jax.numpy as jnp
from jax import lax
from jax.experimental import pallas as pl
from jax.experimental.pallas import tpu as pltpu
from jax.sharding import PartitionSpec as P

MESH = pl.DeviceIdType.MESH
BF = jnp.bfloat16
F32 = jnp.float32

D = 512
HEADS = 8
HEAD_DIM = 64
FF = 2048
SEQ = 512
STEP = 10
ROWS = 4
HALF = D // 2
BLK = D // ROWS
HID = 512

NORM_EPS = 1e-05
BETA_ONE = 0.9
BETA_TWO = 0.999
ADAM_EPS = 1e-08
DECAY_RATE = 0.01
RATE_QKV = 0.03
RATE_PROJ = 0.3
RATE_UP = 0.03
RATE_DOWN = 0.02
RATE_VECTOR = 0.3
VMEM_BYTES = 60 * 2**20

GATHER_UNITS = ((0, 0), (0, 1), (0, 2), (1, 0), (2, 0), (3, 0), (2, 1), (3, 1))
REDUCE_UNITS = ((3, 0), (2, 0), (3, 1), (2, 1), (1, 0), (0, 0), (0, 1), (0, 2))


def at(start, size, multiple=128):
    return pl.ds(pl.multiple_of(start, multiple), size)


def mm(a, b):
    return jnp.dot(a, b, preferred_element_type=F32)


def mm_lt(a, b):
    return lax.dot_general(a, b, (((0,), (0,)), ((), ())), preferred_element_type=F32)


def mm_rt(a, b):
    return lax.dot_general(a, b, (((1,), (1,)), ((), ())), preferred_element_type=F32)


def piece(unit, full, r, c):
    kind, k = unit
    if kind == 0:
        return full[0].at[k, at(r * BLK, BLK), at(c * HALF, HALF)]
    if kind == 1:
        return full[1].at[at(c * HALF, HALF), at(r * BLK, BLK)]
    if kind == 2:
        return full[2].at[at(r * BLK, BLK), at(c * 2 * HID + k * HID, HID)]
    return full[3].at[at(c * 2 * HID + k * HID, HID), at(r * BLK, BLK)]


def own_piece(unit, own):
    kind, k = unit
    if kind == 0:
        return own[0].at[k]
    if kind == 1:
        return own[1]
    if kind == 2:
        return own[2].at[:, pl.ds(k * HID, HID)]
    return own[3].at[pl.ds(k * HID, HID), :]


def column(unit, full, c):
    kind, k = unit
    if kind == 0:
        return full[0].at[k, :, at(c * HALF, HALF)]
    if kind == 1:
        return full[1].at[at(c * HALF, HALF), :]
    if kind == 2:
        return full[2].at[:, at(c * 2 * HID + k * HID, HID)]
    return full[3].at[at(c * 2 * HID + k * HID, HID), :]


def column_shape(unit):
    return ((D, HALF), (HALF, D), (D, HID), (HID, D))[unit[0]]


def piece_shape(unit):
    return ((BLK, HALF), (HALF, BLK), (BLK, HID), (HID, BLK))[unit[0]]


def row_part(unit, col_ref, r):
    if unit[0] in (0, 2):
        return col_ref.at[at(r * BLK, BLK), :]
    return col_ref.at[:, at(r * BLK, BLK)]


def remote(src, dst, send, recv, **where):
    return pltpu.make_async_remote_copy(
        src_ref=src, dst_ref=dst, send_sem=send, recv_sem=recv, device_id=where, device_id_type=MESH
    )


def position():
    return lax.axis_index("row"), lax.axis_index("col")


def flip(r, bit):
    if bit == 1:
        return r + 1 - 2 * lax.rem(r, 2)
    if bit == 2:
        return lax.rem(r + 2, 4)
    return 3 - r


def greet(dp_count):
    r, c = position()
    barrier = pltpu.get_barrier_semaphore()
    peers = [{"col": 1 - c}, {"row": flip(r, 1)}, {"row": flip(r, 2)}]
    if dp_count:
        z = lax.axis_index("dp")
        peers += [{"dp": lax.rem(z + k, dp_count)} for k in range(1, dp_count)]
    for peer in peers:
        pl.semaphore_signal(barrier, inc=1, device_id=peer, device_id_type=MESH)
    pl.semaphore_wait(barrier, len(peers))


def norm_forward(total):
    mean = jnp.mean(total, -1, keepdims=True)
    centered = total - mean
    scale = lax.rsqrt(jnp.mean(centered * centered, -1, keepdims=True) + NORM_EPS)
    return centered * scale, scale


def norm_back(grad, normed, scale, gain):
    scaled = grad * gain
    return scale * (
        scaled - jnp.mean(scaled, -1, keepdims=True) - normed * jnp.mean(scaled * normed, -1, keepdims=True)
    )


def col_sum(value):
    return jnp.sum(value, 0, keepdims=True)


def kernel(dp_count, *refs):
    n = len(REDUCE_UNITS)
    refs = list(refs)

    def take(count):
        out = refs[:count]
        del refs[:count]
        return out

    tok, cot, qkv_in, proj_in, up_in, down_in, vec_in = take(7)
    bo_out, ig_out, gqkv, gproj, gup, gdown, gvec = take(7)
    x_ref, ct_ref, qkv, proj, up, down, vec = take(7)
    own = take(4)
    bo, ig, dqkv, dproj, dup, ddown, vg = take(7)
    q_s, k_s, v_s, p_s, a_s, u_s, gp_s, h1_s, n1_s, da_s, dq_s, dk_s, dv_s = take(13)
    sib_buf, sums, buf_a, buf_b, send_b, zsrc, zbuf = (take(n) for _ in range(7))
    vsum, vbuf, send_in, recv_in, send_g, recv_g, send, recv, send_v, recv_v = take(10)
    full = (qkv, proj, up, down)
    grads, outs = (dqkv, dproj, dup, ddown), (gqkv, gproj, gup, gdown)
    r, c = position()
    sib = 1 - c
    z = lax.axis_index("dp") if dp_count else None
    started, started_end, started_mid = [], [], []
    if dp_count:
        middle = jnp.logical_or(z == 1, z == 2)
        end = jnp.logical_not(middle)

    def go(copy, kept=started):
        copy.start()
        kept.append(copy)
        return copy

    for src, dst in zip((qkv_in, proj_in, up_in, down_in), own):
        dst[...] = src[...].astype(BF)
    greet(dp_count)
    first, across, to_sib = {}, {}, {}

    def issue(u):
        unit = GATHER_UNITS[u]
        src, dst = own_piece(unit, own), piece(unit, full, r, c)
        first[u] = [
            go(remote(src, dst, send_g.at[u, 0], recv_g.at[u, 0], row=flip(r, 1))),
            go(remote(src, dst, send_g.at[u, 1], recv_g.at[u, 1], row=flip(r, 2))),
        ]
        to_sib[u] = [go(remote(src, dst, send_g.at[u, 3], recv_g.at[u, 3], col=sib))]

    def near(u):
        unit = GATHER_UNITS[u]
        for k, bit in ((0, 1), (1, 2)):
            first[u][k].wait_recv()
            block = piece(unit, full, flip(r, bit), c)
            if k == u % 2:
                across[u] = go(remote(block, block, send_g.at[u, 2], recv_g.at[u, 2], row=flip(r, 3 - bit)))
            to_sib[u].append(go(remote(block, block, send_g.at[u, 4 + k], recv_g.at[u, 4 + k], col=sib)))

    def far(u):
        across[u].wait_recv()
        block = piece(GATHER_UNITS[u], full, flip(r, 3), c)
        to_sib[u].append(go(remote(block, block, send_g.at[u, 6], recv_g.at[u, 6], col=sib)))

    def whole(u):
        for copy in to_sib[u]:
            copy.wait_recv()

    ins = [
        go(remote(src.at[at(sib * SEQ, SEQ), :], dst.at[:, at(c * HALF, HALF)], send_in.at[i], recv_in.at[i], col=sib))
        for i, (src, dst) in enumerate(((tok, x_ref), (cot, ct_ref)))
    ]
    ins.append(go(remote(vec_in, vec.at[c], send_in.at[2], recv_in.at[2], col=sib)))
    for u in range(5):
        issue(u)
    for src, dst in ((tok, x_ref), (cot, ct_ref)):
        dst[:, at(c * HALF, HALF)] = src[at(c * SEQ, SEQ), :]
    vec[c] = vec_in[...]
    for unit in GATHER_UNITS:
        piece(unit, full, r, c)[...] = own_piece(unit, own)[...]

    flying = {}

    def wait(key):
        for copy in flying.pop(key):
            copy.wait_recv()

    def add(*views):
        total = views[0][...].astype(F32)
        for view in views[1:]:
            total = total + view[...].astype(F32)
        return total

    def phase(u, step):
        unit = REDUCE_UNITS[u]
        a, b = (1, 2) if u % 2 == 0 else (2, 1)
        out = own_piece(unit, outs)
        if step == 0:
            flying[u] = [go(remote(column(unit, grads, sib), sib_buf[u], send.at[u, 0], recv.at[u, 0], col=sib))]
        elif step == 1:
            wait(u)
            sums[u][...] = add(column(unit, grads, c), sib_buf[u]).astype(BF)
            peer = flip(r, a)
            flying[u] = [
                go(remote(row_part(unit, sums[u], who), buf_a[u].at[i], send.at[u, 1 + i], recv.at[u, 1 + i], row=peer))
                for i, who in ((1, flip(r, 3)), (0, peer))
            ]
        elif step == 2:
            wait(u)
            send_b[u][...] = add(row_part(unit, sums[u], flip(r, b)), buf_a[u].at[1]).astype(BF)
            flying[u] = [go(remote(send_b[u], buf_b[u], send.at[u, 3], recv.at[u, 3], row=flip(r, b)))]
        elif step == 3:
            wait(u)
            total = add(row_part(unit, sums[u], r), buf_a[u].at[0], buf_b[u]).astype(BF)
            if not dp_count:
                out[...] = total
                return
            zsrc[u][...] = total
            side = remote(zsrc[u], zbuf[u].at[0], send.at[u, 4], recv.at[u, 4], dp=flip(z, 1))
            inner = remote(zsrc[u], zbuf[u].at[1], send.at[u, 5], recv.at[u, 5], dp=3 - z)
            back = remote(out, out, send.at[u, 6], recv.at[u, 6], dp=flip(z, 1))
            flying[u] = (side, inner, back)

            @pl.when(end)
            def _():
                go(side, started_end)
        elif dp_count and step == 4:
            side, inner, back = flying[u]

            @pl.when(middle)
            def _():
                side.wait_recv()
                zsrc[u][...] = add(zsrc[u], zbuf[u].at[0]).astype(BF)
                go(inner, started_mid)
        elif dp_count and step == 5:
            side, inner, back = flying[u]

            @pl.when(middle)
            def _():
                inner.wait_recv()
                out[...] = add(zsrc[u], zbuf[u].at[1]).astype(BF)
                go(back, started_mid)
        elif dp_count:
            side, inner, back = flying[u]

            @pl.when(end)
            def _():
                back.wait_recv()

    def vec_step(step):
        if step == 0:
            flying["v"] = [go(remote(vg.at[sib], vbuf.at[0], send_v.at[2], recv_v.at[2], col=sib))]
        elif step == 1:
            wait("v")
            vsum[0] = vg[c] + vbuf[0]
            flying["v"] = [go(remote(vsum.at[0], vbuf.at[1], send_v.at[3], recv_v.at[3], row=flip(r, 1)))]
        elif step == 2:
            wait("v")
            vsum[1] = vsum[0] + vbuf[1]
            flying["v"] = [go(remote(vsum.at[1], vbuf.at[2], send_v.at[4], recv_v.at[4], row=flip(r, 2)))]
        elif step == 3:
            wait("v")
            total = vsum[1] + vbuf[2]
            if not dp_count:
                gvec[...] = total
                return
            vsum[2] = total
            flying["v"] = [
                go(remote(vsum.at[2], vbuf.at[2 + k], send_v.at[4 + k], recv_v.at[4 + k],
                          dp=lax.rem(z + k, dp_count)))
                for k in range(1, dp_count)
            ]
        elif step == 4 and dp_count:
            wait("v")
            parts = [vsum[2]] + [vbuf[2 + k] for k in range(1, dp_count)]
            total = jnp.zeros_like(parts[0])
            for owner in range(dp_count):
                for k, part in enumerate(parts):
                    total = total + jnp.where(lax.rem(z + dp_count - k, dp_count) == owner, part, 0.0)
            gvec[...] = total

    def tick(t):
        for step in (6, 5, 4, 3, 2, 1):
            if 0 <= t - step < n:
                phase(t - step, step)

    def give_back(i, src, dst):
        copy = go(remote(src.at[:, at(sib * HALF, HALF)], dst.at[at(c * SEQ, SEQ), :],
                         send_v.at[i], recv_v.at[i], col=sib))
        dst[at(c * SEQ, SEQ), :] = src[:, at(c * HALF, HALF)]
        return copy

    def row(i):
        return jnp.concatenate([vec[0, i:i + 1, :], vec[1, i:i + 1, :]], 1)

    def put_row(i, value):
        vg[0, i:i + 1, :] = value[:, :HALF]
        vg[1, i:i + 1, :] = value[:, HALF:]

    near(0)
    issue(5)
    near(1)
    far(0)
    issue(6)
    near(2)
    far(1)
    issue(7)
    for copy in ins:
        copy.wait_recv()
    whole(0)
    scaling = HEAD_DIM ** (-0.5)
    q_s[...] = (mm(x_ref[...], qkv[0]) + row(0)).astype(BF)
    far(2)
    whole(1)
    k_s[...] = mm(x_ref[...], qkv[1]).astype(BF)
    near(3)
    whole(2)
    v_s[...] = (mm(x_ref[...], qkv[2]) + row(1)).astype(BF)
    beside = {0: ((far, 3),), 1: ((near, 4),), 3: ((near, 5), (far, 4)), 5: ((near, 6), (far, 5)),
              7: ((near, 7), (far, 6))}
    for h in range(HEADS):
        cols = slice(h * HEAD_DIM, (h + 1) * HEAD_DIM)
        s = mm_rt(q_s[:, cols], k_s[:, cols]) * scaling
        e = jnp.exp(s - jnp.max(s, -1, keepdims=True))
        p = e * (1.0 / jnp.sum(e, -1, keepdims=True))
        p_s[h] = p
        a_s[:, cols] = mm(p.astype(BF), v_s[:, cols]).astype(BF)
        for act, u in beside.get(h, ()):
            act(u)
    whole(3)
    n1, scale1 = norm_forward(x_ref[...].astype(F32) + mm(a_s[...], proj[...]) + row(2))
    n1_s[...] = n1
    h1 = n1 * row(4) + row(5)
    h1_s[...] = h1.astype(BF)
    far(7)
    acc = h1 + row(3)
    for j in (0, 2, 1, 3):
        if j < 2:
            whole(4 + 2 * j)
            whole(5 + 2 * j)
        c_of, k = j // 2, 2 * (j % 2)
        bias = jnp.concatenate([vec[c_of, 8 + k:9 + k, :], vec[c_of, 9 + k:10 + k, :]], 1)
        cols = slice(j * HID, (j + 1) * HID)
        pre = mm(h1_s[...], up[:, cols]) + bias
        half = 0.5 + 0.5 * lax.erf(pre * 0.7071067811865476)
        u = (pre * half).astype(BF)
        u_s[:, cols] = u
        gp_s[:, cols] = half + pre * (0.3989422804014327 * jnp.exp(-0.5 * pre * pre))
        acc = acc + mm(u, down[cols, :])
    n2, scale2 = norm_forward(acc)
    bo[...] = (n2 * row(6) + row(7)).astype(BF)
    give = [give_back(0, bo, bo_out)]

    dy = ct_ref[...].astype(F32)
    put_row(6, col_sum(dy * n2))
    put_row(7, col_sum(dy))
    dr2 = norm_back(dy, n2, scale2, row(6))
    put_row(3, col_sum(dr2))
    g2 = dr2.astype(BF)
    ig[...] = dr2
    for j in (0, 2, 1, 3):
        c_of, k = j // 2, 2 * (j % 2)
        cols = slice(j * HID, (j + 1) * HID)
        ddown[cols, :] = mm_lt(u_s[:, cols], g2).astype(BF)
        if j >= 2:
            phase(2 * (j - 2), 0)
        dz = (mm_rt(g2, down[cols, :]) * gp_s[:, cols]).astype(BF)
        db = col_sum(dz.astype(F32))
        vg[c_of, 8 + k:9 + k, :] = db[:, :HALF]
        vg[c_of, 9 + k:10 + k, :] = db[:, HALF:]
        dup[:, cols] = mm_lt(h1_s[...], dz).astype(BF)
        if j >= 2:
            phase(2 * (j - 2) + 1, 0)
        if j == 3:
            tick(1)
        ig[...] = ig[...] + mm_rt(dz, up[:, cols])
    tick(2)
    acc = ig[...]
    n1 = n1_s[...]
    put_row(4, col_sum(acc * n1))
    put_row(5, col_sum(acc))
    dr1 = norm_back(acc, n1, scale1, row(4))
    put_row(2, col_sum(dr1))
    ig[...] = dr1
    g1 = dr1.astype(BF)
    dproj[...] = mm_lt(a_s[...], g1).astype(BF)
    phase(4, 0)
    da_s[...] = mm_rt(g1, proj[...]).astype(BF)
    tick(3)
    for h in range(HEADS):
        cols = slice(h * HEAD_DIM, (h + 1) * HEAD_DIM)
        da = da_s[:, cols]
        p = p_s[h]
        dp = mm_rt(da, v_s[:, cols])
        ds = (p * (dp - jnp.sum(p * dp, -1, keepdims=True))).astype(BF)
        dq_s[:, cols] = (mm(ds, k_s[:, cols]) * scaling).astype(BF)
        dk_s[:, cols] = (mm_lt(ds, q_s[:, cols]) * scaling).astype(BF)
        dv_s[:, cols] = mm_lt(p.astype(BF), da).astype(BF)
        if h == 2:
            tick(4)
        if h == 5:
            tick(5)
    for i, (src, weight) in enumerate(((dq_s, 0), (dk_s, 1), (dv_s, 2))):
        grad = src[...]
        dqkv[weight] = mm_lt(x_ref[...], grad).astype(BF)
        phase(5 + i, 0)
        if i != 1:
            put_row(i // 2, col_sum(grad.astype(F32)))
    vec_step(0)
    tick(6)
    ig[...] = ig[...] + mm_rt(dq_s[...], qkv[0]) + mm_rt(dk_s[...], qkv[1]) + mm_rt(dv_s[...], qkv[2])
    give.append(give_back(1, ig, ig_out))
    for t in range(7, n + 7):
        tick(t)
        if t <= 10:
            vec_step(t - 6)
    for copy in give:
        copy.wait_recv()
    for copy in started:
        copy.wait_send()
    if dp_count:
        @pl.when(end)
        def _():
            for copy in started_end:
                copy.wait_send()

        @pl.when(middle)
        def _():
            for copy in started_mid:
                copy.wait_send()


def adam_step(weight, mean_old, square_old, gradient, step_rate, decay_rate):
    mean_new = BETA_ONE * mean_old + (1.0 - BETA_ONE) * gradient
    square_new = BETA_TWO * square_old + (1.0 - BETA_TWO) * gradient * gradient
    mean_hat = mean_new / (1.0 - BETA_ONE**STEP)
    square_hat = square_new / (1.0 - BETA_TWO**STEP)
    weight_new = weight - step_rate * (
        mean_hat / (jnp.sqrt(square_hat) + ADAM_EPS) + decay_rate * weight
    )
    return (weight_new, mean_new, square_new)


def shape(dims, dtype):
    return jax.ShapeDtypeStruct(dims, dtype)


def call(kernel, ins, outs, scratch, collective_id=None):
    vmem = pl.BlockSpec(memory_space=pltpu.VMEM)
    extra = {} if collective_id is None else dict(collective_id=collective_id, has_side_effects=True)
    return pl.pallas_call(
        kernel,
        out_shape=outs,
        in_specs=[vmem] * len(ins),
        out_specs=[vmem] * len(outs),
        scratch_shapes=scratch,
        compiler_params=pltpu.CompilerParams(vmem_limit_bytes=VMEM_BYTES, **extra),
    )(*ins)


FULL = ((3, D, D), (D, D), (D, FF), (FF, D))
OWN = ((3, BLK, HALF), (HALF, BLK), (BLK, FF // 2), (FF // 2, BLK))


def body(
    dp_size,
    tokens, cotangent, qkv_weight, proj_weight, up_weight, down_weight, vectors,
    qkv_mean, qkv_square, proj_mean, proj_square, up_mean, up_square,
    down_mean, down_square, vector_mean, vector_square,
):
    dma, vm = pltpu.SemaphoreType.DMA, pltpu.VMEM
    n = len(REDUCE_UNITS)
    dp_count = dp_size if dp_size == 4 else 0
    pieces = [piece_shape(u) for u in REDUCE_UNITS]
    columns = [column_shape(u) for u in REDUCE_UNITS]
    sq, whole = vm((SEQ, D), BF), [vm(s, BF) for s in FULL]
    reduced = call(
        functools.partial(kernel, dp_count),
        (tokens, cotangent, qkv_weight, proj_weight, up_weight, down_weight, vectors),
        [shape((2 * SEQ, HALF), BF), shape((2 * SEQ, HALF), F32)] + [shape(s, BF) for s in OWN]
        + [shape((12, HALF), F32)],
        [sq, sq] + whole + [vm((2, 12, HALF), F32)]
        + [vm(s, BF) for s in OWN]
        + [sq, vm((SEQ, D), F32)] + whole + [vm((2, 12, HALF), F32)]
        + [sq, sq, sq, vm((HEADS, SEQ, SEQ), F32), sq, vm((SEQ, FF), BF), vm((SEQ, FF), F32), sq,
           vm((SEQ, D), F32), sq, sq, sq, sq]
        + [vm(s, BF) for s in columns] * 2
        + [vm((2,) + s, BF) for s in pieces] + [vm(s, BF) for s in pieces] * 3 + [vm((2,) + s, BF) for s in pieces]
        + [vm((3, 12, HALF), F32), vm((6, 12, HALF), F32),
           dma((3,)), dma((3,)), dma((n, 7)), dma((n, 7)), dma((n, 7)), dma((n, 7)), dma((8,)), dma((8,))],
        collective_id=0,
    )
    output, input_grad, grads, vector_grad = reduced[0], reduced[1], reduced[2:6], reduced[6]
    grads = [g.astype(F32) for g in grads]
    if not dp_count:
        grads = [lax.psum(g, "dp") for g in grads]
        vector_grad = lax.psum(vector_grad, "dp")
    return (
        output,
        input_grad,
        *adam_step(qkv_weight, qkv_mean, qkv_square, grads[0], RATE_QKV, DECAY_RATE),
        *adam_step(proj_weight, proj_mean, proj_square, grads[1], RATE_PROJ, DECAY_RATE),
        *adam_step(up_weight, up_mean, up_square, grads[2], RATE_UP, DECAY_RATE),
        *adam_step(down_weight, down_mean, down_square, grads[3], RATE_DOWN, DECAY_RATE),
        *adam_step(vectors, vector_mean, vector_square, vector_grad, RATE_VECTOR, 0.0),
        vector_grad,
    )


def solution(mesh):
    tokens = P(("dp", "row"), "col")
    qkv, proj, up, down, vec = P(None, "row", "col"), P("col", "row"), P("row", "col"), P("col", "row"), P(None, "col")
    return jax.shard_map(
        functools.partial(body, mesh.shape["dp"]),
        mesh=mesh,
        in_specs=(tokens, tokens, qkv, proj, up, down, vec, qkv, qkv, proj, proj, up, up, down, down, vec, vec),
        out_specs=(tokens, tokens) + (qkv,) * 3 + (proj,) * 3 + (up,) * 3 + (down,) * 3 + (vec,) * 4,
        check_vma=False,
    )
```

time: 164 us -> 133 us (0.81)
  Pallas kernels: 152 us -> 122 us
    pallas_call x3 -> x1, Pallas kernels: 152 us -> 122 us  [call(): pl.pallas_call(kernel, out_shape=outs, in_specs=[vmem] * len(ins), out_sp...]
    unnamed x43 -> x45, local copies, waits for them, and re-layouts: 2.97 us -> 3.4 us
where the time goes in v2:
time: 133 us; the launch traced here: 132 us
  Pallas kernels  122 us (92%)
  other arithmetic  6.51 us (5%)
  local copies, waits for them, and re-layouts  3.4 us (3%)
    pallas_call x1, Pallas kernels, call(): pl.pallas_call(kernel, out_shape=outs, in_specs=[vmem] * len(ins), out_sp...  122 us
    sub x5, other arithmetic, adam_step(): weight - step_rate * (mean_hat / (jnp.sqrt(square_hat) + ADAM_EPS) + deca...  6.51 us
    unnamed x45, local copies, waits for them, and re-layouts  3.4 us

profile of v2, /device:TPU:0, one launch (start us, length us, event | category | flops | bytes accessed | tf_op | source)
XLA Modules:
  0.0 132.4 jit_solution(9717120785505374974)
XLA Ops:
  0.7 121.7 %shard_map.304 = (bf16[1024,256]{1,0:T(8,128)(2,1)}, f32[1024,256]{1,0:T(8,128)}, bf16[3,128,256]{2,1,0:T(8,128)(2,1)}, bf16[256,128]{1,0:T(8,128)(2,1)}, bf16[1...) custom-call(bf16[1024,256]{1,0:T(8,128)(2,1)} %refs_0_.1, bf16[1024,256]{1,0:T(8,128)(2,1)} %refs_1_.1, ...), custom_call_target="tpu_custom_call" | custom-call | tf_op jit(solution)/shard_map/pallas_call | solution.py:498
  122.4 0.0 copy-start.5
  122.4 0.0 copy-start.14
  122.4 0.0 copy-start.15
  122.4 0.0 copy-start.6
  122.5 0.0 copy-start.7
  122.5 2.2 %multiply_subtract_fusion.2 = (f32[3,128,256]{2,1,0:T(8,128)}, f32[3,128,256]{2,1,0:T(8,128)}, f32[3,128,256]{2,1,0:T(8,128)}) fusion(f32[3,128,256]{2,1,0:T(8,128)S(1)} %copy-done.2, bf16[3,128,256]{2,1,0:T(8,128)(2,1)} %get-tuple-element.27, f32[3,128,256]{2,1,0:T(8,128)S(1)} %copy-done.10, f32[3,128,256]{2,1,0:T(8,128)S(1)} %copy-done.11), kind=kLoop, calls=%fused_computation.14 | loop fusion | flops 1572864 | bytes 2555904 | tf_op jit(solution)/shard_map/sub | solution.py:485
  124.7 0.0 copy-done.14
  124.7 0.0 copy-done.15
  124.7 0.0 copy-done.18
  124.7 0.0 copy-start.13
  124.7 0.8 multiply_subtract_fusion.3
  125.6 0.3 copy-done
  125.9 0.1 copy-done.13
  126.0 1.4 %multiply_subtract_fusion.1 = (f32[128,1024]{1,0:T(8,128)}, f32[128,1024]{1,0:T(8,128)}, f32[128,1024]{1,0:T(8,128)}) fusion(f32[128,1024]{1,0:T(8,128)S(1)} %copy-done, bf16[128,1024]{1,0:T(8,128)(2,1)S(1)} %copy-done.13, f32[128,1024]{1,0:T(8,128)S(1)} %copy-done.6, f32[128,1024]{1,0:T(8,128)S(1)} %copy-done.7), kind=kLoop, calls=%fused_computation.10 | loop fusion | flops 2097152 | bytes 3407872 | tf_op jit(solution)/shard_map/sub | solution.py:485
  127.4 0.5 copy-done.9
  127.9 0.1 copy-done.12
  128.0 0.0 copy-start.4
  128.0 1.4 %multiply_subtract_fusion = (f32[1024,128]{1,0:T(8,128)}, f32[1024,128]{1,0:T(8,128)}, f32[1024,128]{1,0:T(8,128)}) fusion(f32[1024,128]{1,0:T(8,128)S(1)} %copy-done.1, bf16[1024,128]{1,0:T(8,128)(2,1)S(1)} %copy-done.12, f32[1024,128]{1,0:T(8,128)S(1)} %copy-done.8, f32[1024,128]{1,0:T(8,128)S(1)} %copy-done.9), kind=kLoop, calls=%fused_computation.9 | loop fusion | flops 2097152 | bytes 3407872 | tf_op jit(solution)/shard_map/sub | solution.py:485
  129.4 0.0 copy-done.19
  129.4 0.6 multiply_subtract_fusion.4
  130.0 0.8 copy.38
  130.8 1.0 copy.39
  131.8 0.6 copy.40
  (27 shorter events, 0.1 us)
Async XLA Ops:
  0.7 121.7 %copy-start.2 = (f32[3,128,256]{2,1,0:T(8,128)S(1)}, f32[3,128,256]{2,1,0:T(8,128)}, u32[]{:S(2)}) copy-start(f32[3,128,256]{2,1,0:T(8,128)} %refs_2_.1) | copy-start | bytes 1179652
  0.7 121.7 %copy-start.10 = (f32[3,128,256]{2,1,0:T(8,128)S(1)}, f32[3,128,256]{2,1,0:T(8,128)}, u32[]{:S(2)}) copy-start(f32[3,128,256]{2,1,0:T(8,128)} %param.24) | copy-start | bytes 1179652
  0.7 121.7 %copy-start.11 = (f32[3,128,256]{2,1,0:T(8,128)S(1)}, f32[3,128,256]{2,1,0:T(8,128)}, u32[]{:S(2)}) copy-start(f32[3,128,256]{2,1,0:T(8,128)} %param.25) | copy-start | bytes 1179652
  122.4 2.3 %copy-start.5 = (f32[256,128]{1,0:T(8,128)S(1)}, f32[256,128]{1,0:T(8,128)}, u32[]{:S(2)}) copy-start(f32[256,128]{1,0:T(8,128)} %refs_3_.1) | copy-start | bytes 393220
  122.4 2.3 %copy-start.14 = (f32[256,128]{1,0:T(8,128)S(1)}, f32[256,128]{1,0:T(8,128)}, u32[]{:S(2)}) copy-start(f32[256,128]{1,0:T(8,128)} %param.26) | copy-start | bytes 393220
  122.4 2.3 %copy-start.15 = (f32[256,128]{1,0:T(8,128)S(1)}, f32[256,128]{1,0:T(8,128)}, u32[]{:S(2)}) copy-start(f32[256,128]{1,0:T(8,128)} %param.27) | copy-start | bytes 393220
  122.4 2.3 %copy-start.18 = (bf16[256,128]{1,0:T(8,128)(2,1)S(1)}, bf16[256,128]{1,0:T(8,128)(2,1)}, u32[]{:S(2)}) copy-start(bf16[256,128]{1,0:T(8,128)(2,1)} %get-tuple-element.28) | copy-start | bytes 196612
  122.4 3.1 %copy-start.6 = (f32[128,1024]{1,0:T(8,128)S(1)}, f32[128,1024]{1,0:T(8,128)}, u32[]{:S(2)}) copy-start(f32[128,1024]{1,0:T(8,128)} %param.28) | copy-start | bytes 1572868
  122.5 3.1 %copy-start.7 = (f32[128,1024]{1,0:T(8,128)S(1)}, f32[128,1024]{1,0:T(8,128)}, u32[]{:S(2)}) copy-start(f32[128,1024]{1,0:T(8,128)} %param.29) | copy-start | bytes 1572868
  124.7 1.2 copy-start
  124.7 1.2 copy-start.13
  126.0 1.4 %copy-start.1 = (f32[1024,128]{1,0:T(8,128)S(1)}, f32[1024,128]{1,0:T(8,128)}, u32[]{:S(2)}) copy-start(f32[1024,128]{1,0:T(8,128)} %refs_5_.1) | copy-start | bytes 1572868
  126.0 1.4 %copy-start.8 = (f32[1024,128]{1,0:T(8,128)S(1)}, f32[1024,128]{1,0:T(8,128)}, u32[]{:S(2)}) copy-start(f32[1024,128]{1,0:T(8,128)} %param.30) | copy-start | bytes 1572868
  126.0 1.9 %copy-start.9 = (f32[1024,128]{1,0:T(8,128)S(1)}, f32[1024,128]{1,0:T(8,128)}, u32[]{:S(2)}) copy-start(f32[1024,128]{1,0:T(8,128)} %param.31) | copy-start | bytes 1572868
  126.0 2.0 %copy-start.12 = (bf16[1024,128]{1,0:T(8,128)(2,1)S(1)}, bf16[1024,128]{1,0:T(8,128)(2,1)}, u32[]{:S(2)}) copy-start(bf16[1024,128]{1,0:T(8,128)(2,1)} %get-tuple-element.30) | copy-start | bytes 786436
  127.9 1.4 %copy-start.16 = (f32[12,256]{1,0:T(8,128)S(1)}, f32[12,256]{1,0:T(8,128)}, u32[]{:S(2)}) copy-start(f32[12,256]{1,0:T(8,128)} %refs_6_.1) | copy-start | bytes 36868
  127.9 1.4 %copy-start.17 = (f32[12,256]{1,0:T(8,128)S(1)}, f32[12,256]{1,0:T(8,128)}, u32[]{:S(2)}) copy-start(f32[12,256]{1,0:T(8,128)} %get-tuple-element.82) | copy-start | bytes 36868
  127.9 1.4 %copy-start.19 = (f32[12,256]{1,0:T(8,128)S(1)}, f32[12,256]{1,0:T(8,128)}, u32[]{:S(2)}) copy-start(f32[12,256]{1,0:T(8,128)} %param.32) | copy-start | bytes 36868
  127.9 1.4 %copy-start.20 = (f32[12,256]{1,0:T(8,128)S(1)}, f32[12,256]{1,0:T(8,128)}, u32[]{:S(2)}) copy-start(f32[12,256]{1,0:T(8,128)} %param.33) | copy-start | bytes 36868
  128.0 2.1 %copy-start.4 = (bf16[1024,256]{1,0:T(8,128)(2,1)S(1)}, bf16[1024,256]{1,0:T(8,128)(2,1)}, u32[]{:S(2)}) copy-start(bf16[1024,256]{1,0:T(8,128)(2,1)} %get-tuple-element.65) | copy-start | bytes 1572868
  129.4 1.5 %copy-start.3 = (f32[1024,256]{1,0:T(8,128)S(1)}, f32[1024,256]{1,0:T(8,128)}, u32[]{:S(2)}) copy-start(f32[1024,256]{1,0:T(8,128)} %get-tuple-element.66) | copy-start | bytes 3145732

commit v3 on v2

--- a/solution.py
+++ b/solution.py
@@ -35,6 +35,7 @@
 VMEM_BYTES = 60 * 2**20
 
 GATHER_UNITS = ((0, 0), (0, 1), (0, 2), (1, 0), (2, 0), (3, 0), (2, 1), (3, 1))
+LEAD = {4: 0, 5: 1, 6: 1, 7: 0}
 REDUCE_UNITS = ((3, 0), (2, 0), (3, 1), (2, 1), (1, 0), (0, 0), (0, 1), (0, 2))
 
 
@@ -184,41 +185,91 @@
     for src, dst in zip((qkv_in, proj_in, up_in, down_in), own):
         dst[...] = src[...].astype(BF)
     greet(dp_count)
-    first, across, to_sib = {}, {}, {}
+    hops = {}
+    started_lead = ([], [])
+    if dp_count:
+        parity = lax.rem(z, 2)
+
+    def shared(u):
+        return bool(dp_count) and u in LEAD
+
+    def hop(u, slot, who, **where):
+        unit = GATHER_UNITS[u]
+        block = piece(unit, full, who, c)
+        src = own_piece(unit, own) if slot in (0, 1, 3) else block
+        return remote(src, block, send_g.at[u, slot], recv_g.at[u, slot], **where)
 
     def issue(u):
-        unit = GATHER_UNITS[u]
-        src, dst = own_piece(unit, own), piece(unit, full, r, c)
-        first[u] = [
-            go(remote(src, dst, send_g.at[u, 0], recv_g.at[u, 0], row=flip(r, 1))),
-            go(remote(src, dst, send_g.at[u, 1], recv_g.at[u, 1], row=flip(r, 2))),
-        ]
-        to_sib[u] = [go(remote(src, dst, send_g.at[u, 3], recv_g.at[u, 3], col=sib))]
+        x, y, far_row = flip(r, 1), flip(r, 2), flip(r, 3)
+        hops[u] = {
+            0: hop(u, 0, r, row=x),
+            1: hop(u, 1, r, row=y),
+            2: hop(u, 2, x if u % 2 == 0 else y, row=y if u % 2 == 0 else x),
+            3: hop(u, 3, r, col=sib),
+            4: hop(u, 4, x, col=sib),
+            5: hop(u, 5, y, col=sib),
+            6: hop(u, 6, far_row, col=sib),
+        }
+        go(hops[u][3])
+        if not shared(u):
+            go(hops[u][0])
+            go(hops[u][1])
+            return
+        for k, who in enumerate((x, y, far_row)):
+            hops[u][7 + k] = hop(u, 7 + k, who, dp=flip(z, 1))
+
+        @pl.when(parity == LEAD[u])
+        def _():
+            go(hops[u][0], started_lead[LEAD[u]])
+            go(hops[u][1], started_lead[LEAD[u]])
+
+    def lead(u, act):
+        if not shared(u):
+            act(started)
+        else:
+            @pl.when(parity == LEAD[u])
+            def _():
+                act(started_lead[LEAD[u]])
 
     def near(u):
-        unit = GATHER_UNITS[u]
-        for k, bit in ((0, 1), (1, 2)):
-            first[u][k].wait_recv()
-            block = piece(unit, full, flip(r, bit), c)
-            if k == u % 2:
-                across[u] = go(remote(block, block, send_g.at[u, 2], recv_g.at[u, 2], row=flip(r, 3 - bit)))
-            to_sib[u].append(go(remote(block, block, send_g.at[u, 4 + k], recv_g.at[u, 4 + k], col=sib)))
+        def act(kept):
+            for k in (0, 1):
+                hops[u][k].wait_recv()
+                if k == u % 2:
+                    go(hops[u][2], kept)
+                if shared(u):
+                    go(hops[u][7 + k], kept)
+                go(hops[u][4 + k], kept)
+
+        lead(u, act)
 
     def far(u):
-        across[u].wait_recv()
-        block = piece(GATHER_UNITS[u], full, flip(r, 3), c)
-        to_sib[u].append(go(remote(block, block, send_g.at[u, 6], recv_g.at[u, 6], col=sib)))
+        def act(kept):
+            hops[u][2].wait_recv()
+            if shared(u):
+                go(hops[u][9], kept)
+            go(hops[u][6], kept)
+
+        lead(u, act)
+
+    def follow(u):
+        if shared(u):
+            @pl.when(parity != LEAD[u])
+            def _():
+                for k in range(3):
+                    hops[u][7 + k].wait_recv()
+                    go(hops[u][4 + k], started_lead[1 - LEAD[u]])
 
     def whole(u):
-        for copy in to_sib[u]:
-            copy.wait_recv()
+        for slot in (3, 4, 5, 6):
+            hops[u][slot].wait_recv()
 
     ins = [
         go(remote(src.at[at(sib * SEQ, SEQ), :], dst.at[:, at(c * HALF, HALF)], send_in.at[i], recv_in.at[i], col=sib))
         for i, (src, dst) in enumerate(((tok, x_ref), (cot, ct_ref)))
     ]
     ins.append(go(remote(vec_in, vec.at[c], send_in.at[2], recv_in.at[2], col=sib)))
-    for u in range(5):
+    for u in range(6):
         issue(u)
     for src, dst in ((tok, x_ref), (cot, ct_ref)):
         dst[:, at(c * HALF, HALF)] = src[at(c * SEQ, SEQ), :]
@@ -326,10 +377,9 @@
                     total = total + jnp.where(lax.rem(z + dp_count - k, dp_count) == owner, part, 0.0)
             gvec[...] = total
 
-    def tick(t):
-        for step in (6, 5, 4, 3, 2, 1):
-            if 0 <= t - step < n:
-                phase(t - step, step)
+    def stage(group, step):
+        phase(2 * group, step)
+        phase(2 * group + 1, step)
 
     def give_back(i, src, dst):
         copy = go(remote(src.at[:, at(sib * HALF, HALF)], dst.at[at(c * SEQ, SEQ), :],
@@ -345,13 +395,12 @@
         vg[1, i:i + 1, :] = value[:, HALF:]
 
     near(0)
-    issue(5)
+    issue(6)
     near(1)
     far(0)
-    issue(6)
+    issue(7)
     near(2)
     far(1)
-    issue(7)
     for copy in ins:
         copy.wait_recv()
     whole(0)
@@ -363,8 +412,8 @@
     near(3)
     whole(2)
     v_s[...] = (mm(x_ref[...], qkv[2]) + row(1)).astype(BF)
-    beside = {0: ((far, 3),), 1: ((near, 4),), 3: ((near, 5), (far, 4)), 5: ((near, 6), (far, 5)),
-              7: ((near, 7), (far, 6))}
+    beside = {0: ((far, 3),), 1: ((near, 4), (near, 5)), 3: ((far, 4), (far, 5)), 5: ((follow, 4), (follow, 5)),
+              7: ((near, 6), (near, 7))}
     for h in range(HEADS):
         cols = slice(h * HEAD_DIM, (h + 1) * HEAD_DIM)
         s = mm_rt(q_s[:, cols], k_s[:, cols]) * scaling
@@ -379,9 +428,13 @@
     n1_s[...] = n1
     h1 = n1 * row(4) + row(5)
     h1_s[...] = h1.astype(BF)
+    far(6)
     far(7)
     acc = h1 + row(3)
     for j in (0, 2, 1, 3):
+        if j == 1:
+            follow(6)
+            follow(7)
         if j < 2:
             whole(4 + 2 * j)
             whole(5 + 2 * j)
@@ -418,10 +471,9 @@
         dup[:, cols] = mm_lt(h1_s[...], dz).astype(BF)
         if j >= 2:
             phase(2 * (j - 2) + 1, 0)
-        if j == 3:
-            tick(1)
+        if j == 1:
+            stage(0, 1)
         ig[...] = ig[...] + mm_rt(dz, up[:, cols])
-    tick(2)
     acc = ig[...]
     n1 = n1_s[...]
     put_row(4, col_sum(acc * n1))
@@ -433,7 +485,6 @@
     dproj[...] = mm_lt(a_s[...], g1).astype(BF)
     phase(4, 0)
     da_s[...] = mm_rt(g1, proj[...]).astype(BF)
-    tick(3)
     for h in range(HEADS):
         cols = slice(h * HEAD_DIM, (h + 1) * HEAD_DIM)
         da = da_s[:, cols]
@@ -443,10 +494,14 @@
         dq_s[:, cols] = (mm(ds, k_s[:, cols]) * scaling).astype(BF)
         dk_s[:, cols] = (mm_lt(ds, q_s[:, cols]) * scaling).astype(BF)
         dv_s[:, cols] = mm_lt(p.astype(BF), da).astype(BF)
-        if h == 2:
-            tick(4)
-        if h == 5:
-            tick(5)
+        if h == 0:
+            stage(0, 2)
+            stage(1, 1)
+        if h == 3:
+            stage(0, 3)
+        if h == 7:
+            stage(1, 2)
+            stage(0, 4)
     for i, (src, weight) in enumerate(((dq_s, 0), (dk_s, 1), (dv_s, 2))):
         grad = src[...]
         dqkv[weight] = mm_lt(x_ref[...], grad).astype(BF)
@@ -454,18 +509,35 @@
         if i != 1:
             put_row(i // 2, col_sum(grad.astype(F32)))
     vec_step(0)
-    tick(6)
+    stage(2, 1)
+    stage(1, 3)
+    stage(0, 5)
     ig[...] = ig[...] + mm_rt(dq_s[...], qkv[0]) + mm_rt(dk_s[...], qkv[1]) + mm_rt(dv_s[...], qkv[2])
     give.append(give_back(1, ig, ig_out))
-    for t in range(7, n + 7):
-        tick(t)
-        if t <= 10:
-            vec_step(t - 6)
+    tail = (
+        ((2, 2), (3, 1), (1, 4), (0, 6)),
+        ((2, 3), (3, 2), (1, 5)),
+        ((2, 4), (3, 3), (1, 6)),
+        ((2, 5), (3, 4)),
+        ((2, 6), (3, 5)),
+        ((3, 6),),
+    )
+    for t, group in enumerate(tail):
+        for pair in group:
+            stage(*pair)
+        if t < 4:
+            vec_step(t + 1)
     for copy in give:
         copy.wait_recv()
     for copy in started:
         copy.wait_send()
     if dp_count:
+        for side in (0, 1):
+            @pl.when(parity == side)
+            def _():
+                for copy in started_lead[side]:
+                    copy.wait_send()
+
         @pl.when(end)
         def _():
             for copy in started_end:
@@ -534,7 +606,7 @@
         + [vm(s, BF) for s in columns] * 2
         + [vm((2,) + s, BF) for s in pieces] + [vm(s, BF) for s in pieces] * 3 + [vm((2,) + s, BF) for s in pieces]
         + [vm((3, 12, HALF), F32), vm((6, 12, HALF), F32),
-           dma((3,)), dma((3,)), dma((n, 7)), dma((n, 7)), dma((n, 7)), dma((n, 7)), dma((8,)), dma((8,))],
+           dma((3,)), dma((3,)), dma((n, 10)), dma((n, 10)), dma((n, 7)), dma((n, 7)), dma((8,)), dma((8,))],
         collective_id=0,
     )
     output, input_grad, grads, vector_grad = reduced[0], reduced[1], reduced[2:6], reduced[6]

time: 133 us -> 118 us (0.89)
  Pallas kernels: 122 us -> 108 us
    pallas_call x1, Pallas kernels: 122 us -> 108 us  [call(): pl.pallas_call(kernel, out_shape=outs, in_specs=[vmem] * len(ins), out_sp...]
where the time goes in v3:
time: 118 us
  Pallas kernels  108 us (92%)
  other arithmetic  6.51 us (6%)
  local copies, waits for them, and re-layouts  3.4 us (3%)
    pallas_call x1, Pallas kernels, call(): pl.pallas_call(kernel, out_shape=outs, in_specs=[vmem] * len(ins), out_sp...  108 us
    sub x5, other arithmetic, adam_step(): weight - step_rate * (mean_hat / (jnp.sqrt(square_hat) + ADAM_EPS) + deca...  6.51 us
    unnamed x45, local copies, waits for them, and re-layouts  3.4 us

profile of v3, /device:TPU:0, one launch (start us, length us, event | category | flops | bytes accessed | tf_op | source)
XLA Modules:
  0.0 118.3 jit_solution(661400630160664563)
XLA Ops:
  0.7 107.5 %shard_map.304 = (bf16[1024,256]{1,0:T(8,128)(2,1)}, f32[1024,256]{1,0:T(8,128)}, bf16[3,128,256]{2,1,0:T(8,128)(2,1)}, bf16[256,128]{1,0:T(8,128)(2,1)}, bf16[1...) custom-call(bf16[1024,256]{1,0:T(8,128)(2,1)} %refs_0_.1, bf16[1024,256]{1,0:T(8,128)(2,1)} %refs_1_.1, ...), custom_call_target="tpu_custom_call" | custom-call | tf_op jit(solution)/shard_map/pallas_call | solution.py:570
  108.2 0.0 copy-done.2
  108.2 0.0 copy-done.10
  108.2 0.0 copy-done.11
  108.2 0.0 copy-start.5
  108.3 0.0 copy-start.14
  108.3 0.0 copy-start.15
  108.3 0.0 copy-start.6
  108.3 0.0 copy-start.7
  108.3 2.2 %multiply_subtract_fusion.2 = (f32[3,128,256]{2,1,0:T(8,128)}, f32[3,128,256]{2,1,0:T(8,128)}, f32[3,128,256]{2,1,0:T(8,128)}) fusion(f32[3,128,256]{2,1,0:T(8,128)S(1)} %copy-done.2, bf16[3,128,256]{2,1,0:T(8,128)(2,1)} %get-tuple-element.27, f32[3,128,256]{2,1,0:T(8,128)S(1)} %copy-done.10, f32[3,128,256]{2,1,0:T(8,128)S(1)} %copy-done.11), kind=kLoop, calls=%fused_computation.14 | loop fusion | flops 1572864 | bytes 2555904 | tf_op jit(solution)/shard_map/sub | solution.py:557
  110.5 0.0 copy-done.5
  110.6 0.8 multiply_subtract_fusion.3
  111.4 0.3 copy-done
  111.7 0.1 copy-done.13
  111.8 1.4 %multiply_subtract_fusion.1 = (f32[128,1024]{1,0:T(8,128)}, f32[128,1024]{1,0:T(8,128)}, f32[128,1024]{1,0:T(8,128)}) fusion(f32[128,1024]{1,0:T(8,128)S(1)} %copy-done, bf16[128,1024]{1,0:T(8,128)(2,1)S(1)} %copy-done.13, f32[128,1024]{1,0:T(8,128)S(1)} %copy-done.6, f32[128,1024]{1,0:T(8,128)S(1)} %copy-done.7), kind=kLoop, calls=%fused_computation.10 | loop fusion | flops 2097152 | bytes 3407872 | tf_op jit(solution)/shard_map/sub | solution.py:557
  113.2 0.0 copy-done.8
  113.2 0.5 copy-done.9
  113.7 0.1 copy-done.12
  113.8 1.4 %multiply_subtract_fusion = (f32[1024,128]{1,0:T(8,128)}, f32[1024,128]{1,0:T(8,128)}, f32[1024,128]{1,0:T(8,128)}) fusion(f32[1024,128]{1,0:T(8,128)S(1)} %copy-done.1, bf16[1024,128]{1,0:T(8,128)(2,1)S(1)} %copy-done.12, f32[1024,128]{1,0:T(8,128)S(1)} %copy-done.8, f32[1024,128]{1,0:T(8,128)S(1)} %copy-done.9), kind=kLoop, calls=%fused_computation.9 | loop fusion | flops 2097152 | bytes 3407872 | tf_op jit(solution)/shard_map/sub | solution.py:557
  115.2 0.0 copy-done.17
  115.2 0.6 multiply_subtract_fusion.4
  115.9 0.8 copy.38
  116.7 1.0 copy.39
  117.6 0.6 copy.40
  (27 shorter events, 0.1 us)
Async XLA Ops:
  0.7 107.6 %copy-start.2 = (f32[3,128,256]{2,1,0:T(8,128)S(1)}, f32[3,128,256]{2,1,0:T(8,128)}, u32[]{:S(2)}) copy-start(f32[3,128,256]{2,1,0:T(8,128)} %refs_2_.1) | copy-start | bytes 1179652
  0.7 107.6 %copy-start.10 = (f32[3,128,256]{2,1,0:T(8,128)S(1)}, f32[3,128,256]{2,1,0:T(8,128)}, u32[]{:S(2)}) copy-start(f32[3,128,256]{2,1,0:T(8,128)} %param.24) | copy-start | bytes 1179652
  0.7 107.6 %copy-start.11 = (f32[3,128,256]{2,1,0:T(8,128)S(1)}, f32[3,128,256]{2,1,0:T(8,128)}, u32[]{:S(2)}) copy-start(f32[3,128,256]{2,1,0:T(8,128)} %param.25) | copy-start | bytes 1179652
  108.2 2.3 %copy-start.5 = (f32[256,128]{1,0:T(8,128)S(1)}, f32[256,128]{1,0:T(8,128)}, u32[]{:S(2)}) copy-start(f32[256,128]{1,0:T(8,128)} %refs_3_.1) | copy-start | bytes 393220
  108.3 2.3 %copy-start.14 = (f32[256,128]{1,0:T(8,128)S(1)}, f32[256,128]{1,0:T(8,128)}, u32[]{:S(2)}) copy-start(f32[256,128]{1,0:T(8,128)} %param.26) | copy-start | bytes 393220
  108.3 2.3 %copy-start.15 = (f32[256,128]{1,0:T(8,128)S(1)}, f32[256,128]{1,0:T(8,128)}, u32[]{:S(2)}) copy-start(f32[256,128]{1,0:T(8,128)} %param.27) | copy-start | bytes 393220
  108.3 2.3 %copy-start.18 = (bf16[256,128]{1,0:T(8,128)(2,1)S(1)}, bf16[256,128]{1,0:T(8,128)(2,1)}, u32[]{:S(2)}) copy-start(bf16[256,128]{1,0:T(8,128)(2,1)} %get-tuple-element.28) | copy-start | bytes 196612
  108.3 3.1 %copy-start.6 = (f32[128,1024]{1,0:T(8,128)S(1)}, f32[128,1024]{1,0:T(8,128)}, u32[]{:S(2)}) copy-start(f32[128,1024]{1,0:T(8,128)} %param.28) | copy-start | bytes 1572868
  108.3 3.1 %copy-start.7 = (f32[128,1024]{1,0:T(8,128)S(1)}, f32[128,1024]{1,0:T(8,128)}, u32[]{:S(2)}) copy-start(f32[128,1024]{1,0:T(8,128)} %param.29) | copy-start | bytes 1572868
  110.5 1.2 copy-start
  110.6 1.2 %copy-start.13 = (bf16[128,1024]{1,0:T(8,128)(2,1)S(1)}, bf16[128,1024]{1,0:T(8,128)(2,1)}, u32[]{:S(2)}) copy-start(bf16[128,1024]{1,0:T(8,128)(2,1)} %get-tuple-element.29) | copy-start | bytes 786436
  111.8 1.4 %copy-start.1 = (f32[1024,128]{1,0:T(8,128)S(1)}, f32[1024,128]{1,0:T(8,128)}, u32[]{:S(2)}) copy-start(f32[1024,128]{1,0:T(8,128)} %refs_5_.1) | copy-start | bytes 1572868
  111.8 1.4 %copy-start.8 = (f32[1024,128]{1,0:T(8,128)S(1)}, f32[1024,128]{1,0:T(8,128)}, u32[]{:S(2)}) copy-start(f32[1024,128]{1,0:T(8,128)} %param.30) | copy-start | bytes 1572868
  111.8 1.9 %copy-start.9 = (f32[1024,128]{1,0:T(8,128)S(1)}, f32[1024,128]{1,0:T(8,128)}, u32[]{:S(2)}) copy-start(f32[1024,128]{1,0:T(8,128)} %param.31) | copy-start | bytes 1572868
  111.8 2.0 %copy-start.12 = (bf16[1024,128]{1,0:T(8,128)(2,1)S(1)}, bf16[1024,128]{1,0:T(8,128)(2,1)}, u32[]{:S(2)}) copy-start(bf16[1024,128]{1,0:T(8,128)(2,1)} %get-tuple-element.30) | copy-start | bytes 786436
  113.8 1.4 %copy-start.16 = (f32[12,256]{1,0:T(8,128)S(1)}, f32[12,256]{1,0:T(8,128)}, u32[]{:S(2)}) copy-start(f32[12,256]{1,0:T(8,128)} %refs_6_.1) | copy-start | bytes 36868
  113.8 1.4 %copy-start.17 = (f32[12,256]{1,0:T(8,128)S(1)}, f32[12,256]{1,0:T(8,128)}, u32[]{:S(2)}) copy-start(f32[12,256]{1,0:T(8,128)} %get-tuple-element.82) | copy-start | bytes 36868
  113.8 1.4 %copy-start.19 = (f32[12,256]{1,0:T(8,128)S(1)}, f32[12,256]{1,0:T(8,128)}, u32[]{:S(2)}) copy-start(f32[12,256]{1,0:T(8,128)} %param.32) | copy-start | bytes 36868
  113.8 1.4 %copy-start.20 = (f32[12,256]{1,0:T(8,128)S(1)}, f32[12,256]{1,0:T(8,128)}, u32[]{:S(2)}) copy-start(f32[12,256]{1,0:T(8,128)} %param.33) | copy-start | bytes 36868
  113.8 2.1 %copy-start.4 = (bf16[1024,256]{1,0:T(8,128)(2,1)S(1)}, bf16[1024,256]{1,0:T(8,128)(2,1)}, u32[]{:S(2)}) copy-start(bf16[1024,256]{1,0:T(8,128)(2,1)} %get-tuple-element.65) | copy-start | bytes 1572868
  115.2 1.5 %copy-start.3 = (f32[1024,256]{1,0:T(8,128)S(1)}, f32[1024,256]{1,0:T(8,128)}, u32[]{:S(2)}) copy-start(f32[1024,256]{1,0:T(8,128)} %get-tuple-element.66) | copy-start | bytes 3145732
